TPU v7x, 32 devices: a whole 2x2x4 slice. The times are simulated.
32 devices in a mesh: fsdp: 16 (over z, y, core), rep: 2 (over x).
Axes of the slice: x: 2, y: 2, z: 4, core: 2. Of those that a mesh axis runs over, the one named last changes fastest.
Arguments:
- tokens: bfloat16 [32768, 1024], P(('fsdp', 'rep')), may hold values from -6 to 6
- segment_ids: int32 [32768], P(('fsdp', 'rep')), may hold values from 0 to 47, as said below
- in_weight: bfloat16 [1024, 4384], P(('fsdp', 'rep')), may hold values from -0.1875 to 0.1875
- out_weight: bfloat16 [2048, 1024], P(None, ('fsdp', 'rep')), may hold values from -0.125 to 0.125
- conv_weight: bfloat16 [4, 2304], P(None, ('fsdp', 'rep')), may hold values from -4 to 4
- conv_bias: bfloat16 [2304], P(('fsdp', 'rep')), may hold values from -3 to 3
- norm_gain: bfloat16 [1024], P(('fsdp', 'rep')), may hold values from 0.5 to 1.5
- gate_gain: bfloat16 [2048], P(('fsdp', 'rep')), may hold values from 0.5 to 1.5
- step_bias: float32 [32], replicated, may hold values from -4 to -2
- decay_log: float32 [32], replicated, may hold values from -4 to 0
- skip_gain: float32 [32], replicated, may hold values from 0.5 to 2
- cotangent: bfloat16 [32768, 1024], P(('fsdp', 'rep')), may hold values from -6 to 6
Outputs:
- mixed: bfloat16 [32768, 1024], P(('fsdp', 'rep'))
- grad_tokens: bfloat16 [32768, 1024], P(('fsdp', 'rep'))
- grad_in_weight: float32 [1024, 4384], P(('fsdp', 'rep'))
- grad_out_weight: float32 [2048, 1024], P(None, ('fsdp', 'rep'))
- grad_conv_weight: float32 [4, 2304], P(None, ('fsdp', 'rep'))
- grad_conv_bias: float32 [2304], P(('fsdp', 'rep'))
- grad_norm_gain: float32 [1024], P(('fsdp', 'rep'))
- grad_gate_gain: float32 [2048], P(('fsdp', 'rep'))
- grad_step_bias: float32 [32], replicated
- grad_decay_log: float32 [32], replicated
- grad_skip_gain: float32 [32], replicated
Inputs may be any that keep to these rules, and one draw needn't show every extreme that they name: `segment_ids`: segment ids never fall and are numbered 0, 1, 2, ... in order; every device's block of 1024 tokens begins a new segment and no segment crosses the end of such a block; the first block is one whole segment; of the other blocks exactly (32768 // 1024) // 2 hold two segments, the second beginning at a multiple of 64 no earlier than 256 and no later than 768 tokens into the block, and the rest hold one.
All inputs are finite; a program needn't handle non-finite values.
Results may differ from a plain program's by a relative error of at most 0.0057.
Values may be sent and summed in bfloat16 or wider, within the bound.
A program may use at most 256 MiB of HBM per device.

v0:
```python
import jax
import jax.numpy as jnp
from jax import lax
from jax.sharding import PartitionSpec as P

SPAN = 256


epsilon = 1e-05


def span_scan(
    head_flat, step_size, log_rate, input_map, output_map, seg_rows, span_len, head_count
):
    tok_count, inner_size = head_flat.shape
    head_size = inner_size // head_count
    state_size = input_map.shape[1]
    block_count = tok_count // span_len
    highest = lax.Precision.HIGHEST

    def to_spans(values):
        return values.reshape((block_count, span_len) + values.shape[1:])

    def span_step(carried, pieces):
        state_held, prior_seg = carried
        flat_part, size_part, rate_part, in_part, out_part, seg_part = pieces
        x_part = flat_part.reshape(span_len, head_count, head_size)
        cumul = jnp.cumsum(rate_part, axis=0)
        cumul_t = cumul.T
        log_gap = cumul_t[:, :, None] - cumul_t[:, None, :]
        rows_idx = lax.broadcasted_iota(jnp.int32, (span_len, span_len), 0)
        cols_idx = lax.broadcasted_iota(jnp.int32, (span_len, span_len), 1)
        same_seg = (seg_part[:, None] == seg_part[None, :]) & (rows_idx >= cols_idx)
        decay_mask = jnp.where(same_seg[None, :, :], jnp.exp(jnp.minimum(log_gap, 0.0)), 0.0)
        scores = jnp.dot(out_part, in_part.T, precision=highest)
        scaled_x = x_part * size_part[:, :, None]
        inside = jnp.einsum("hts,ts,shp->thp", decay_mask, scores, scaled_x, precision=highest)
        entering = (seg_part == prior_seg).astype(x_part.dtype)
        carried_in = jnp.einsum("tn,hpn->thp", out_part, state_held, precision=highest)
        carried_in = carried_in * (jnp.exp(cumul) * entering[:, None])[:, :, None]
        final_seg = seg_part[span_len - 1]
        tail_decay = (
            jnp.exp(cumul[span_len - 1][None, :] - cumul)
            * (seg_part == final_seg).astype(x_part.dtype)[:, None]
        )
        keep_rate = jnp.exp(cumul[span_len - 1]) * (final_seg == prior_seg).astype(x_part.dtype)
        state_held = keep_rate[:, None, None] * state_held + jnp.einsum(
            "sh,sn,shp->hpn", tail_decay, in_part, scaled_x, precision=highest
        )
        return ((state_held, final_seg), (inside + carried_in).reshape(span_len, inner_size))

    start_state = (
        jnp.zeros((head_count, head_size, state_size), head_flat.dtype),
        jnp.array(-1, jnp.int32),
    )
    pieces = tuple(
        (
            to_spans(values)
            for values in (head_flat, step_size, log_rate, input_map, output_map, seg_rows)
        )
    )
    unused, outputs = lax.scan(jax.checkpoint(span_step), start_state, pieces)
    return outputs.reshape(tok_count, inner_size)


def mixer(
    proj, conv_weight, conv_bias, step_bias, decay_log, skip_gain, gate_gain, seg_rows, span_len
):
    inner_size = gate_gain.shape[0]
    head_count = step_bias.shape[0]
    width_xbc = conv_weight.shape[1]
    conv_size = conv_weight.shape[0]
    state_size = (width_xbc - inner_size) // 2
    head_size = inner_size // head_count
    tok_count = proj.shape[0]
    gate_in = proj[:, :inner_size]
    conv_in = proj[:, inner_size : inner_size + width_xbc]
    step_raw = proj[:, inner_size + width_xbc :]
    padded = jnp.concatenate([jnp.zeros((conv_size - 1, width_xbc), proj.dtype), conv_in], 0)
    seg_pad = jnp.concatenate([jnp.full((conv_size - 1,), -1, jnp.int32), seg_rows], 0)
    conv_pre = conv_bias + conv_weight[conv_size - 1] * conv_in
    for offset in range(1, conv_size):
        begin = conv_size - 1 - offset
        earlier = padded[begin : begin + tok_count]
        same_seg = (seg_pad[begin : begin + tok_count] == seg_rows).astype(proj.dtype)
        conv_pre = conv_pre + conv_weight[conv_size - 1 - offset] * earlier * same_seg[:, None]
    conv_out = jax.nn.silu(conv_pre)
    head_flat = conv_out[:, :inner_size]
    input_map = conv_out[:, inner_size : inner_size + state_size]
    output_map = conv_out[:, inner_size + state_size :]
    step_size = jax.nn.softplus(step_raw + step_bias)
    log_rate = -step_size * jnp.exp(decay_log)
    scan_out = span_scan(
        head_flat, step_size, log_rate, input_map, output_map, seg_rows, span_len, head_count
    )
    skip_wide = jnp.repeat(skip_gain, head_size)
    scan_out = scan_out + skip_wide[None, :] * head_flat
    gated = scan_out * jax.nn.silu(gate_in)
    return gated * lax.rsqrt(jnp.mean(gated * gated, -1, keepdims=True) + epsilon) * gate_gain


def rms_rows(values, gain):
    return values * lax.rsqrt(jnp.mean(values * values, -1, keepdims=True) + epsilon) * gain


def local(
    tokens,
    segment_ids,
    in_weight,
    out_weight,
    conv_weight,
    conv_bias,
    norm_gain,
    gate_gain,
    step_bias,
    decay_log,
    skip_gain,
    cotangent,
):
    gathered = (
        lax.all_gather(in_weight, ("fsdp", "rep"), axis=0, tiled=True),
        lax.all_gather(out_weight, ("fsdp", "rep"), axis=1, tiled=True),
        lax.all_gather(conv_weight, ("fsdp", "rep"), axis=1, tiled=True),
        lax.all_gather(conv_bias, ("fsdp", "rep"), axis=0, tiled=True),
        lax.all_gather(norm_gain, ("fsdp", "rep"), axis=0, tiled=True),
        lax.all_gather(gate_gain, ("fsdp", "rep"), axis=0, tiled=True),
    )
    in_full, out_full, conv_full, bias_full, norm_full, gate_full = gathered
    hidden_in = tokens.astype(jnp.float32)
    normed, norm_pullback = jax.vjp(rms_rows, hidden_in, norm_full.astype(jnp.float32))
    normed_low = normed.astype(jnp.bfloat16)
    proj = jnp.dot(normed_low, in_full, preferred_element_type=jnp.float32)

    def mixer_local(
        proj_rows, conv_taps, conv_shift, step_shift, decay_rates, skip_rates, gate_scale
    ):
        return mixer(
            proj_rows,
            conv_taps,
            conv_shift,
            step_shift,
            decay_rates,
            skip_rates,
            gate_scale,
            segment_ids,
            SPAN,
        )

    gated_out, mixer_pullback = jax.vjp(
        mixer_local,
        proj,
        conv_full.astype(jnp.float32),
        bias_full.astype(jnp.float32),
        step_bias,
        decay_log,
        skip_gain,
        gate_full.astype(jnp.float32),
    )
    gated_low = gated_out.astype(jnp.bfloat16)
    branch = jnp.dot(gated_low, out_full, preferred_element_type=jnp.float32)
    mixed = (hidden_in + branch).astype(jnp.bfloat16)
    in_back, out_back = (
        lax.all_gather(in_weight, ("fsdp", "rep"), axis=0, tiled=True),
        lax.all_gather(out_weight, ("fsdp", "rep"), axis=1, tiled=True),
    )
    grad_out_w = lax.dot_general(
        gated_low, cotangent, (((0,), (0,)), ((), ())), preferred_element_type=jnp.float32
    )
    grad_gated = lax.dot_general(
        cotangent, out_back, (((1,), (1,)), ((), ())), preferred_element_type=jnp.float32
    )
    grad_proj, grad_conv_w, grad_conv_b, grad_step, grad_decay, grad_skip, grad_gate = (
        mixer_pullback(grad_gated)
    )
    grad_proj_low = grad_proj.astype(jnp.bfloat16)
    grad_in_w = lax.dot_general(
        normed_low, grad_proj_low, (((0,), (0,)), ((), ())), preferred_element_type=jnp.float32
    )
    grad_normed = lax.dot_general(
        grad_proj_low, in_back, (((1,), (1,)), ((), ())), preferred_element_type=jnp.float32
    )
    grad_hidden, grad_norm = norm_pullback(grad_normed)
    grad_tokens = (cotangent.astype(jnp.float32) + grad_hidden).astype(jnp.bfloat16)
    shares = (
        lax.psum_scatter(grad_in_w, ("fsdp", "rep"), scatter_dimension=0, tiled=True),
        lax.psum_scatter(grad_out_w, ("fsdp", "rep"), scatter_dimension=1, tiled=True),
        lax.psum_scatter(grad_conv_w, ("fsdp", "rep"), scatter_dimension=1, tiled=True),
        lax.psum_scatter(grad_conv_b, ("fsdp", "rep"), scatter_dimension=0, tiled=True),
        lax.psum_scatter(grad_norm, ("fsdp", "rep"), scatter_dimension=0, tiled=True),
        lax.psum_scatter(grad_gate, ("fsdp", "rep"), scatter_dimension=0, tiled=True),
    )
    head_totals = lax.psum((grad_step, grad_decay, grad_skip), ("fsdp", "rep"))
    return (
        mixed,
        grad_tokens,
        shares[0],
        shares[1],
        shares[2],
        shares[3],
        shares[4],
        shares[5],
        head_totals[0],
        head_totals[1],
        head_totals[2],
    )


def solution(mesh):
    in_specs = (
        P(("fsdp", "rep"), None),
        P(("fsdp", "rep")),
        P(("fsdp", "rep"), None),
        P(None, ("fsdp", "rep")),
        P(None, ("fsdp", "rep")),
        P(("fsdp", "rep")),
        P(("fsdp", "rep")),
        P(("fsdp", "rep")),
        P(),
        P(),
        P(),
        P(("fsdp", "rep"), None),
    )
    out_specs = (
        P(("fsdp", "rep"), None),
        P(("fsdp", "rep"), None),
        P(("fsdp", "rep"), None),
        P(None, ("fsdp", "rep")),
        P(None, ("fsdp", "rep")),
        P(("fsdp", "rep")),
        P(("fsdp", "rep")),
        P(("fsdp", "rep")),
        P(),
        P(),
        P(),
    )
    return jax.shard_map(local, mesh=mesh, in_specs=in_specs, out_specs=out_specs, check_vma=False)
```

profile of v0, /device:TPU:0, one launch (start us, length us, event | category | flops | bytes accessed | tf_op | source)
XLA Modules:
  0.0 1685.7 jit_solution(15243201175300052777)
XLA Ops:
  15.7 42.4 %all-reduce.25 = (bf16[1024]{0:T(1024)(128)(2,1)S(1)}, bf16[2304]{0:T(1024)(128)(2,1)S(1)}, bf16[2048]{0:T(1024)(128)(2,1)S(1)}) all-reduce(bf16[1024]{0:T(1024)(128)(2,1)S(1)} %dynamic-update-slice, bf16[2304]{0:T(1024)(128)(2,1)S(1)} %dynamic-update-slice.1, ...), channel_id=1, replica_groups=mesh['fsdp'=16,'rep'=2] {'fsdp','rep'}, use_global_device_ids=true, to_apply=%add.17 | all-reduce | flops 5376 | bytes 21504
  59.0 67.2 %all-gather = bf16[32,72,4]{1,2,0:T(4,128)(2,1)S(1)} all-gather(bf16[1,72,4]{1,2,0:T(4,128)(2,1)} %bitcast.407), channel_id=1, replica_groups=mesh['fsdp'=16,'rep'=2] {'fsdp','rep'}, dimensions={0}, use_global_device_ids=true | all-gather | bytes 19008 | tf_op jit(solution)/shard_map/all_gather | solution.py:123
  126.5 17.6 %fusion.119 = f32[1024,4384]{0,1:T(8,128)} fusion(bf16[1024,4384]{1,0:T(8,128)(2,1)} %all-gather.4.cloned.1.call-done, bf16[1024,1024]{1,0:T(8,128)(2,1)} %param.16, f32[1024]{0:T(1024)S(1)} %convert_element_type.93, f32[1024]{0:T(1024)S(1)} %fusion.130), kind=kOutput, calls=%fused_computation.195 | convolution fusion | flops 9198108672 | bytes 29040640 | tf_op jit(solution)/shard_map/dot_general | solution.py:132
  148.9 11.5 fusion.102
  182.3 322.5 %while.45 = (s32[]{:T(128)}, f32[32,64,128]{2,1,0:T(8,128)S(1)}, s32[]{:T(128)}, f32[4,256,2048]{1,0,2:T(4,128)}, f32[4,32,64,128]{3,2,1,0:T(8,128)}, /*index=5*...) while((s32[]{:T(128)}, f32[32,64,128]{2,1,0:T(8,128)S(1)}, ...), condition=%wide.region_4.5_spmd.clone, body=%wide.region_1.4_spmd.clone.sunk | while | flops 3335488512 | bytes 30060692 | solution.py:62
  191.6 10.1 fusion.214
  217.3 45.1 %dynamic_update_slice.85 = f32[4,256,2048]{1,0,2:T(4,128)} dynamic-update-slice(f32[4,256,2048]{1,0,2:T(4,128)} %get-tuple-element.1141, f32[1,256,2048]{1,0,2:T(1,128)S(1)} %copy.332, s32[]{:T(128)S(6)} %copy.365, s32[]{:T(128)} %constant.139.clone.1..sunk, s32[]{:T(128)} %constant.139.clone.1..sunk) | dynamic-update-slice | bytes 4194308 | tf_op jit(solution)/shard_map/jvp()/while/body/jit(dynamic_update_index_in_dim)/dynamic_update_slice | solution.py:62
  272.1 10.1 fusion.214
  297.8 45.1 %dynamic_update_slice.85 = f32[4,256,2048]{1,0,2:T(4,128)} dynamic-update-slice(f32[4,256,2048]{1,0,2:T(4,128)} %get-tuple-element.1141, f32[1,256,2048]{1,0,2:T(1,128)S(1)} %copy.332, s32[]{:T(128)S(6)} %copy.365, s32[]{:T(128)} %constant.139.clone.1..sunk, s32[]{:T(128)} %constant.139.clone.1..sunk) | dynamic-update-slice | bytes 4194308 | tf_op jit(solution)/shard_map/jvp()/while/body/jit(dynamic_update_index_in_dim)/dynamic_update_slice | solution.py:62
  378.2 45.1 %dynamic_update_slice.85 = f32[4,256,2048]{1,0,2:T(4,128)} dynamic-update-slice(f32[4,256,2048]{1,0,2:T(4,128)} %get-tuple-element.1141, f32[1,256,2048]{1,0,2:T(1,128)S(1)} %copy.332, s32[]{:T(128)S(6)} %copy.365, s32[]{:T(128)} %constant.139.clone.1..sunk, s32[]{:T(128)} %constant.139.clone.1..sunk) | dynamic-update-slice | bytes 4194308 | tf_op jit(solution)/shard_map/jvp()/while/body/jit(dynamic_update_index_in_dim)/dynamic_update_slice | solution.py:62
  458.7 45.1 %dynamic_update_slice.85 = f32[4,256,2048]{1,0,2:T(4,128)} dynamic-update-slice(f32[4,256,2048]{1,0,2:T(4,128)} %get-tuple-element.1141, f32[1,256,2048]{1,0,2:T(1,128)S(1)} %copy.332, s32[]{:T(128)S(6)} %copy.365, s32[]{:T(128)} %constant.139.clone.1..sunk, s32[]{:T(128)} %constant.139.clone.1..sunk) | dynamic-update-slice | bytes 4194308 | tf_op jit(solution)/shard_map/jvp()/while/body/jit(dynamic_update_index_in_dim)/dynamic_update_slice | solution.py:62
  510.4 10.5 multiply_reduce_fusion.11
  531.3 12.4 multiply_reduce_fusion.9
  543.8 21.6 %multiply_reduce_fusion.8 = (f32[2048]{0:T(1024)}, f32[1024,2048]{0,1:T(8,128)}, f32[1024,2048]{0,1:T(8,128)}) fusion(f32[1024,2304]{0,1:T(8,128)} %copy-done.1, f32[1024,4384]{0,1:T(8,128)} %fusion.119, f32[1024,2048]{0,1:T(8,128)} %copy-done.5, f32[1024]{0:T(1024)S(1)} %multiply_multiply_fusion.5, f32[1024]{0:T(1024)S(1)} %fusion.131, ...), kind=kLoop, calls=%fused_computation.168 | loop fusion | flops 44038144 | bytes 58753024 | tf_op jit(solution)/shard_map/transpose(jvp())/reduce_sum | solution.py:97
  565.4 10.6 reshape.484
  583.0 619.3 %while.46 = (s32[]{:T(128)}, f32[32,64,128]{2,1,0:T(8,128)}, f32[4,256,2048]{1,0,2:T(4,128)}, f32[4,256,32]{1,0,2:T(4,128)}, f32[4,256,32]{1,0,2:T(4,128)}, /*in...) while((s32[]{:T(128)}, f32[32,64,128]{2,1,0:T(8,128)}, ...), condition=%wide.region_18.19_spmd.clone, body=%wide.region_7.18_spmd.clone.sunk | while | flops 7605371904 | bytes 90062744 | solution.py:62
  646.5 15.5 fusion.236
  690.0 45.1 %dynamic_update_slice.89 = f32[4,256,2048]{1,0,2:T(4,128)} dynamic-update-slice(f32[4,256,2048]{1,0,2:T(4,128)} %get-tuple-element.1192, f32[1,256,2048]{1,0,2:T(1,128)S(1)} %copy-done, s32[]{:T(128)S(6)} %sub.268, s32[]{:T(128)} %constant.139.clone.1..sunk.1, s32[]{:T(128)} %constant.139.clone.1..sunk.1) | dynamic-update-slice | bytes 4194308 | tf_op jit(solution)/shard_map/transpose(jvp())/while/body/jit(dynamic_update_index_in_dim)/dynamic_update_slice | solution.py:62
  799.6 15.5 fusion.236
  843.0 45.1 %dynamic_update_slice.89 = f32[4,256,2048]{1,0,2:T(4,128)} dynamic-update-slice(f32[4,256,2048]{1,0,2:T(4,128)} %get-tuple-element.1192, f32[1,256,2048]{1,0,2:T(1,128)S(1)} %copy-done, s32[]{:T(128)S(6)} %sub.268, s32[]{:T(128)} %constant.139.clone.1..sunk.1, s32[]{:T(128)} %constant.139.clone.1..sunk.1) | dynamic-update-slice | bytes 4194308 | tf_op jit(solution)/shard_map/transpose(jvp())/while/body/jit(dynamic_update_index_in_dim)/dynamic_update_slice | solution.py:62
  952.5 15.5 fusion.236
  996.0 45.1 %dynamic_update_slice.89 = f32[4,256,2048]{1,0,2:T(4,128)} dynamic-update-slice(f32[4,256,2048]{1,0,2:T(4,128)} %get-tuple-element.1192, f32[1,256,2048]{1,0,2:T(1,128)S(1)} %copy-done, s32[]{:T(128)S(6)} %sub.268, s32[]{:T(128)} %constant.139.clone.1..sunk.1, s32[]{:T(128)} %constant.139.clone.1..sunk.1) | dynamic-update-slice | bytes 4194308 | tf_op jit(solution)/shard_map/transpose(jvp())/while/body/jit(dynamic_update_index_in_dim)/dynamic_update_slice | solution.py:62
  1105.5 15.5 fusion.236
  1149.0 45.1 %dynamic_update_slice.89 = f32[4,256,2048]{1,0,2:T(4,128)} dynamic-update-slice(f32[4,256,2048]{1,0,2:T(4,128)} %get-tuple-element.1192, f32[1,256,2048]{1,0,2:T(1,128)S(1)} %copy-done, s32[]{:T(128)S(6)} %sub.268, s32[]{:T(128)} %constant.139.clone.1..sunk.1, s32[]{:T(128)} %constant.139.clone.1..sunk.1) | dynamic-update-slice | bytes 4194308 | tf_op jit(solution)/shard_map/transpose(jvp())/while/body/jit(dynamic_update_index_in_dim)/dynamic_update_slice | solution.py:62
  1217.7 26.7 %multiply_reduce_fusion.7 = (f32[2304]{0:T(1024)S(1)}, f32[2304]{0:T(1024)S(1)}, f32[2304]{0:T(1024)S(1)}, f32[2304]{0:T(1024)S(1)}, f32[2304]{0:T(1024)S(1)}, /*index=5*/f32[1024,2304]{0,1:T(8,128)}) fusion(f32[1024,2304]{0,1:T(8,128)} %copy-done.3, f32[1024]{0:T(1024)S(1)} %copy-done.26, f32[1024]{0:T(1024)S(1)} %copy-done.28, f32[1024]{0:T(1024)S(1)} %copy-done.24, ...), kind=kLoop, calls=%fused_computation.158 | loop fusion | flops 54252288 | bytes 47244288 | tf_op jit(solution)/shard_map/transpose(jvp())/reduce_sum | solution.py:86
  1244.4 13.9 multiply_multiply_fusion.3
  1258.3 14.7 fusion.101
  1273.1 18.3 %fusion.117 = f32[1024,4384]{1,0:T(8,128)} fusion(bf16[1024,1024]{1,0:T(8,128)(2,1)S(1)} %copy-done.8, f32[1024]{0:T(1024)S(1)} %copy-done.37, f32[1024]{0:T(1024)S(1)} %copy-done.35, f32[1024,2048]{0,1:T(8,128)} %get-tuple-element.870, f32[1024,2304]{0,1:T(8,128)} %fusion.101, f32[1024,32]{0,1:T(8,128)S(1)} %get-tuple-element.842), kind=kOutput, calls=%fused_computation.194 | convolution fusion | flops 9211576320 | bytes 38019072 | tf_op jit(solution)/shard_map/dot_general | solution.py:176
  1292.4 18.6 %fusion.109 = (f32[1024]{0:T(1024)S(1)}, f32[1024]{0:T(1024)S(1)}, f32[1024,1024]{1,0:T(8,128)}) fusion(bf16[1024,1024]{1,0:T(8,128)(2,1)S(1)} %copy-done.8, f32[1024]{0:T(1024)S(1)} %copy-done.35, f32[1024]{0:T(1024)S(1)} %copy-done.37, bf16[1024,4384]{1,0:T(8,128)(2,1)} %all-gather.4.cloned.1.call-done, f32[1024,2048]{0,1:T(8,128)} %get-tuple-element.870, ...), kind=kOutput, calls=%fused_computation.186 | convolution fusion | flops 9214720000 | bytes 33243136 | tf_op jit(solution)/shard_map/dot_general | solution.py:179
  1311.0 40.6 %all-reduce.24 = (f32[4,2304]{1,0:T(4,128)S(1)}, f32[2304]{0:T(1024)S(1)}, f32[1024]{0:T(1024)S(1)}, f32[2048]{0:T(1024)S(1)}, f32[32]{0:T(128)}, /*index=5*/f32[32]{0:T(128)}, f32[32]{0:T(128)}) all-reduce(f32[4,2304]{1,0:T(4,128)S(1)} %pad_add_fusion.2, ...), channel_id=4, replica_groups=mesh['fsdp'=16,'rep'=2] {'fsdp','rep'}, use_global_device_ids=true, to_apply=%region_26.27.clone | all-reduce | flops 14688 | bytes 117504
  1358.6 10.1 fusion.113
  1368.8 310.1 %reduce-scatter.4.cloned.1.call-done = f32[32,4384]{1,0:T(8,128)} async-done(((f32[1024,4384]{1,0:T(8,128)}), f32[32,4384]{1,0:T(8,128)}) %reduce-scatter.4.cloned.1.call-update) | async-done | bytes 561168 | tf_op jit(solution)/shard_map/reduce_scatter | solution.py:185
  (486 shorter events, 560.7 us)
Async XLA Ops:
  7.2 119.3 %all-gather.4.cloned.1.call-start = ((), (), s32[]{:S(2)}) async-start(), calls=%async_computation.2 | async-start | bytes 9461760 | tf_op jit(solution)/shard_map/all_gather | solution.py:121
  7.9 523.4 %all-gather.6.cloned.1.call-start = ((), (), s32[]{:S(2)}) async-start(), calls=%async_computation.3 | async-start | bytes 4325376 | tf_op jit(solution)/shard_map/all_gather | solution.py:122
  8.7 1360.1 %reduce-scatter.6.cloned.1.call-start = ((), (), s32[]{:S(2)}) async-start(), calls=%async_computation.5 | async-start | bytes 8650752 | tf_op jit(solution)/shard_map/reduce_scatter | solution.py:186
  10.3 138.5 %copy-start.23 = (f32[1024]{0:T(1024)}, f32[1024]{0:T(1024)S(1)}, u32[]{:S(2)}) copy-start(f32[1024]{0:T(1024)S(1)} %get-tuple-element.877) | copy-start | bytes 12292
  10.3 138.5 %copy-start.25 = (f32[1024]{0:T(1024)}, f32[1024]{0:T(1024)S(1)}, u32[]{:S(2)}) copy-start(f32[1024]{0:T(1024)S(1)} %get-tuple-element.878) | copy-start | bytes 12292
  10.3 138.5 %copy-start.27 = (f32[1024]{0:T(1024)}, f32[1024]{0:T(1024)S(1)}, u32[]{:S(2)}) copy-start(f32[1024]{0:T(1024)S(1)} %get-tuple-element.879) | copy-start | bytes 12292
  11.0 165.0 %copy-start.43 = (f32[32]{0:T(128)}, f32[32]{0:T(128)S(1)}, u32[]{:S(2)}) copy-start(f32[32]{0:T(128)S(1)} %exp.93) | copy-start | bytes 388
  13.1 45.0 %copy-start.29 = (f32[1024]{0:T(1024)}, f32[1024]{0:T(1024)S(1)}, u32[]{:S(2)}) copy-start(f32[1024]{0:T(1024)S(1)} %fusion.112) | copy-start | bytes 12292
  13.1 130.9 %copy-start.34 = (f32[1024]{0:T(1024)}, f32[1024]{0:T(1024)S(1)}, u32[]{:S(2)}) copy-start(f32[1024]{0:T(1024)S(1)} %fusion.130) | copy-start | bytes 12292
  58.1 85.9 %copy-start.36 = (f32[1024]{0:T(1024)}, f32[1024]{0:T(1024)S(1)}, u32[]{:S(2)}) copy-start(f32[1024]{0:T(1024)S(1)} %convert_element_type.93) | copy-start | bytes 12292
  58.2 485.6 %copy-start.32 = (f32[2048]{0:T(1024)}, f32[2048]{0:T(1024)S(1)}, u32[]{:S(2)}) copy-start(f32[2048]{0:T(1024)S(1)} %convert_element_type.100) | copy-start | bytes 24580
  59.0 484.8 %copy-start.13 = (f32[2048]{0:T(1024)}, f32[2048]{0:T(1024)S(1)}, u32[]{:S(2)}) copy-start(f32[2048]{0:T(1024)S(1)} %mul.670) | copy-start | bytes 24580
  126.4 22.4 %copy-start.15 = (f32[2304]{0:T(1024)}, f32[2304]{0:T(1024)S(1)}, u32[]{:S(2)}) copy-start(f32[2304]{0:T(1024)S(1)} %get-tuple-element.769) | copy-start | bytes 27652
  126.5 22.4 %copy-start.17 = (f32[2304]{0:T(1024)}, f32[2304]{0:T(1024)S(1)}, u32[]{:S(2)}) copy-start(f32[2304]{0:T(1024)S(1)} %get-tuple-element.770) | copy-start | bytes 27652
  126.5 22.4 %copy-start.19 = (f32[2304]{0:T(1024)}, f32[2304]{0:T(1024)S(1)}, u32[]{:S(2)}) copy-start(f32[2304]{0:T(1024)S(1)} %get-tuple-element.771) | copy-start | bytes 27652
  126.5 22.4 %copy-start.21 = (f32[2304]{0:T(1024)}, f32[2304]{0:T(1024)S(1)}, u32[]{:S(2)}) copy-start(f32[2304]{0:T(1024)S(1)} %get-tuple-element.772) | copy-start | bytes 27652
  520.9 22.9 %copy-start.38 = (f32[1024]{0:T(1024)}, f32[1024]{0:T(1024)S(1)}, u32[]{:S(2)}) copy-start(f32[1024]{0:T(1024)S(1)} %fusion.131) | copy-start | bytes 12292
  543.7 1135.2 %reduce-scatter.4.cloned.1.call-start = ((), (), s32[]{:S(2)}) async-start(), calls=%async_computation.4 | async-start | bytes 18923520 | tf_op jit(solution)/shard_map/reduce_scatter | solution.py:185
  668.6 20.2 %copy-start.6 = (f32[256,128]{1,0:T(8,128)S(1)}, f32[256,128]{1,0:T(8,128)}, u32[]{:S(2)}) copy-start(f32[256,128]{1,0:T(8,128)} %fusion.241) | copy-start | bytes 393220 | tf_op jit(solution)/shard_map/transpose(jvp())/while
  821.7 20.1 %copy-start.6 = (f32[256,128]{1,0:T(8,128)S(1)}, f32[256,128]{1,0:T(8,128)}, u32[]{:S(2)}) copy-start(f32[256,128]{1,0:T(8,128)} %fusion.241) | copy-start | bytes 393220 | tf_op jit(solution)/shard_map/transpose(jvp())/while
  974.6 20.1 %copy-start.6 = (f32[256,128]{1,0:T(8,128)S(1)}, f32[256,128]{1,0:T(8,128)}, u32[]{:S(2)}) copy-start(f32[256,128]{1,0:T(8,128)} %fusion.241) | copy-start | bytes 393220 | tf_op jit(solution)/shard_map/transpose(jvp())/while
  1127.6 20.1 %copy-start.6 = (f32[256,128]{1,0:T(8,128)S(1)}, f32[256,128]{1,0:T(8,128)}, u32[]{:S(2)}) copy-start(f32[256,128]{1,0:T(8,128)} %fusion.241) | copy-start | bytes 393220 | tf_op jit(solution)/shard_map/transpose(jvp())/while
  1217.7 26.7 %copy-start.18 = (f32[2304]{0:T(1024)S(1)}, f32[2304]{0:T(1024)}, u32[]{:S(2)}) copy-start(f32[2304]{0:T(1024)} %copy-done.17) | copy-start | bytes 27652
  1217.7 26.7 %copy-start.20 = (f32[2304]{0:T(1024)S(1)}, f32[2304]{0:T(1024)}, u32[]{:S(2)}) copy-start(f32[2304]{0:T(1024)} %copy-done.19) | copy-start | bytes 27652
  1217.7 26.7 %copy-start.22 = (f32[2304]{0:T(1024)S(1)}, f32[2304]{0:T(1024)}, u32[]{:S(2)}) copy-start(f32[2304]{0:T(1024)} %copy-done.21) | copy-start | bytes 27652
  1258.3 14.8 copy-start.8
  1258.3 14.8 copy-start.35
  1258.3 14.8 copy-start.37
  1292.4 18.6 %copy-start.40 = (f32[2048]{0:T(1024)S(1)}, f32[2048]{0:T(1024)}, u32[]{:S(2)}) copy-start(f32[2048]{0:T(1024)} %get-tuple-element.763) | copy-start | bytes 24580
  1292.4 61.6 %copy-start.30 = (f32[1024]{0:T(1024)S(1)}, f32[1024]{0:T(1024)}, u32[]{:S(2)}) copy-start(f32[1024]{0:T(1024)} %copy-done.29) | copy-start | bytes 12292
  1311.0 47.6 %copy-start.33 = (f32[2048]{0:T(1024)S(1)}, f32[2048]{0:T(1024)}, u32[]{:S(2)}) copy-start(f32[2048]{0:T(1024)} %copy-done.32) | copy-start | bytes 24580
  1311.0 47.6 %copy-start.39 = (f32[1024]{0:T(1024)S(1)}, f32[1024]{0:T(1024)}, u32[]{:S(2)}) copy-start(f32[1024]{0:T(1024)} %copy-done.38) | copy-start | bytes 12292
  (33 other events, 278.0 us)
Sparse Core Ops, SparseCore 0:
  10.8 83.7 all-gather.3
  97.6 60.7 all-gather.5
  543.9 179.0 reduce-scatter.5
  1291.6 387.2 reduce-scatter.3
where the time goes:
time: 1700 us; the launch traced here: 1690 us
  local copies, waits for them, and re-layouts  644 us (38%)
  matrix products  343 us (20%)
  waiting for transfers between devices  312 us (18%)
  other arithmetic  201 us (12%)
  blocking collectives  150 us (9%)
  loops' own time  20.3 us (1%)
    dynamic_update_slice x36, local copies, waits for them, and re-layouts, span_scan(): unused, outputs = lax.scan(jax.checkpoint(span_step), start_state, pieces)  456 us
    reduce_scatter x1, waiting for transfers between devices, local(): lax.psum_scatter(grad_in_w, ('fsdp', 'rep'), scatter_dimension=0, tiled=T...  310 us
    dot_general x12, matrix products, span_step(): jnp.einsum('hts,ts,shp->thp', decay_mask, scores, scaled_x, precision=hig...  141 us
    unnamed x2, blocking collectives  83.1 us
    all_gather x1, blocking collectives, local(): lax.all_gather(conv_weight, ('fsdp', 'rep'), axis=1, tiled=True)  67.2 us
    dot_general x16, matrix products, span_step(): jnp.einsum('tn,hpn->thp', out_part, state_held, precision=highest)  59 us
    dot_general x12, matrix products, span_step(): jnp.einsum('sh,sn,shp->hpn', tail_decay, in_part, scaled_x, precision=hig...  42.4 us
  transfers between devices with their start and end apart: 4, of which 1 were waited for; matrix products, arithmetic and copies ran while one was open for 69% of the time, Pallas kernels for 0%

commit v1 on v0

v1 whole, which is shorter than its diff:
```python
import functools

import jax
import jax.numpy as jnp
from jax import lax
from jax.experimental import pallas as pl
from jax.experimental.pallas import tpu as pltpu
from jax.sharding import PartitionSpec as P

CHUNK = 128
F32 = jnp.float32
BF16 = jnp.bfloat16
epsilon = 1e-05


def dot_at(a, b, a_dim, b_dim):
    return lax.dot_general(
        a.astype(BF16), b.astype(BF16), (((a_dim,), (b_dim,)), ((), ())), preferred_element_type=F32
    )


def two_part(values, table, table_dim):
    high = values.astype(BF16)
    low = (values - high.astype(F32)).astype(BF16)
    return dot_at(high, table, 1, table_dim) + dot_at(low, table, 1, table_dim)


def chunk_mask(seg_col, seg_row):
    size = seg_col.shape[0]
    rows = lax.broadcasted_iota(jnp.int32, (size, size), 0)
    cols = lax.broadcasted_iota(jnp.int32, (size, size), 1)
    return (seg_col == seg_row) & (rows >= cols)


def scan_kernel(
    u_ref, b_ref, c_ref, cum_ref, cumt_ref, din_ref, dout_ref, keep_ref, segc_ref, segr_ref, table_ref,
    y_ref, held_ref, state_ref,
):
    @pl.when(pl.program_id(0) == 0)
    def _():
        state_ref[...] = jnp.zeros_like(state_ref)

    table = table_ref[...]
    b_part, c_part = b_ref[...], c_ref[...]
    mask = chunk_mask(segc_ref[...], segr_ref[...])
    scores = jnp.where(mask, dot_at(c_part, b_part, 1, 1), 0.0)
    state = state_ref[...]
    state_low = state.astype(BF16)
    held_ref[0] = state_low
    y_ref[...] = dot_at(c_part, state_low, 1, 0) * two_part(din_ref[...], table, 0)
    cum, cumt = cum_ref[...], cumt_ref[...]
    size = cum.shape[0]
    heads = cum.shape[1]
    first = lax.broadcasted_iota(jnp.int32, (size, 128), 1) < 64
    for pair in range(heads // 2):
        lanes = slice(pair * 128, pair * 128 + 128)
        u_low = u_ref[:, lanes].astype(BF16)
        parts = []
        for head in (2 * pair, 2 * pair + 1):
            gap = cum[:, head : head + 1] - cumt[head : head + 1, :]
            parts.append(dot_at(scores * jnp.exp(jnp.minimum(gap, 0.0)), u_low, 1, 0))
        y_ref[:, lanes] += jnp.where(first, parts[0], parts[1])
    keep_wide = two_part(keep_ref[0], table, 0)[:1]
    weighted = u_ref[...] * two_part(dout_ref[...], table, 0)
    state_ref[...] = state * keep_wide + dot_at(b_part, weighted, 0, 0)


def scan_back_kernel(
    u_ref, b_ref, c_ref, cum_ref, cumt_ref, din_ref, dout_ref, keep_ref, segc_ref, segr_ref, table_ref,
    held_ref, dy_ref,
    du_ref, db_ref, dc_ref, drow_ref, dcol_ref, ddin_ref, ddout_ref, dkeep_ref, dstate_ref,
):
    @pl.when(pl.program_id(0) == 0)
    def _():
        dstate_ref[...] = jnp.zeros_like(dstate_ref)

    table = table_ref[...]
    b_part, c_part = b_ref[...].astype(BF16), c_ref[...].astype(BF16)
    mask = chunk_mask(segc_ref[...], segr_ref[...])
    scores = jnp.where(mask, dot_at(c_part, b_part, 1, 1), 0.0)
    state_low = held_ref[0]
    dstate = dstate_ref[...]
    dstate_low = dstate.astype(BF16)
    u_all, dy_all = u_ref[...], dy_ref[...]
    in_wide = two_part(din_ref[...], table, 0)
    out_wide = two_part(dout_ref[...], table, 0)
    keep_wide = two_part(keep_ref[0], table, 0)[:1]
    carried = dot_at(c_part, state_low, 1, 0)
    ddin_ref[...] = two_part(dy_all * carried, table, 1)
    sent = dot_at(b_part, dstate_low, 1, 0)
    ddout_ref[...] = two_part(u_all * sent, table, 1)
    du_ref[...] = sent * out_wide
    dkeep = jnp.sum(dstate * state_low.astype(F32), axis=0, keepdims=True)
    dkeep_ref[0] = two_part(jnp.broadcast_to(dkeep, (8, dkeep.shape[1])), table, 1)
    dy_in = (dy_all * in_wide).astype(BF16)
    u_out = (u_all * out_wide).astype(BF16)
    dc_carry = dot_at(dy_in, state_low, 1, 1)
    db_carry = dot_at(u_out, dstate_low, 1, 1)
    dstate_ref[...] = dstate * keep_wide + dot_at(c_part, dy_in, 0, 0)
    cum, cumt = cum_ref[...], cumt_ref[...]
    size = cum.shape[0]
    heads = cum.shape[1]
    first = lax.broadcasted_iota(jnp.int32, (size, 128), 1) < 64
    dscores = jnp.zeros((size, size), F32)
    for pair in range(heads // 2):
        lanes = slice(pair * 128, pair * 128 + 128)
        u_low = u_ref[:, lanes].astype(BF16)
        dy_pair = dy_ref[:, lanes]
        dy_low = dy_pair.astype(BF16)
        parts = []
        for side, head in enumerate((2 * pair, 2 * pair + 1)):
            gap = cum[:, head : head + 1] - cumt[head : head + 1, :]
            decay = jnp.exp(jnp.minimum(gap, 0.0))
            mixing = scores * decay
            parts.append(dot_at(mixing, dy_low, 0, 0))
            own = jnp.where(first if side == 0 else jnp.logical_not(first), dy_pair, 0.0)
            dmix = dot_at(own, u_low, 1, 1)
            dscores = dscores + dmix * decay
            weights = dmix * mixing
            drow_ref[:, head : head + 1] = jnp.sum(weights, axis=1, keepdims=True)
            dcol_ref[head : head + 1, :] = jnp.sum(weights, axis=0, keepdims=True)
        du_ref[:, lanes] += jnp.where(first, parts[0], parts[1])
    dscores = jnp.where(mask, dscores, 0.0)
    dc_ref[...] = dc_carry + dot_at(dscores, b_part, 1, 0)
    db_ref[...] = db_carry + dot_at(dscores, c_part, 0, 0)


def scan_specs(count, inner, heads, states, order):
    return [
        pl.BlockSpec((CHUNK, inner), lambda i: (order(i), 0)),
        pl.BlockSpec((CHUNK, states), lambda i: (order(i), 0)),
        pl.BlockSpec((CHUNK, states), lambda i: (order(i), 0)),
        pl.BlockSpec((CHUNK, heads), lambda i: (order(i), 0)),
        pl.BlockSpec((heads, CHUNK), lambda i: (0, order(i))),
        pl.BlockSpec((CHUNK, heads), lambda i: (order(i), 0)),
        pl.BlockSpec((CHUNK, heads), lambda i: (order(i), 0)),
        pl.BlockSpec((1, 8, heads), lambda i: (order(i), 0, 0)),
        pl.BlockSpec((CHUNK, 1), lambda i: (order(i), 0)),
        pl.BlockSpec((1, CHUNK), lambda i: (0, order(i))),
        pl.BlockSpec((heads, inner), lambda i: (0, 0)),
    ]


def scan_forward(pieces):
    u = pieces[0]
    toks, inner = u.shape
    states, heads = pieces[1].shape[1], pieces[3].shape[1]
    count = toks // CHUNK
    return pl.pallas_call(
        scan_kernel,
        grid=(count,),
        in_specs=scan_specs(count, inner, heads, states, lambda i: i),
        out_specs=[
            pl.BlockSpec((CHUNK, inner), lambda i: (i, 0)),
            pl.BlockSpec((1, states, inner), lambda i: (i, 0, 0)),
        ],
        out_shape=[
            jax.ShapeDtypeStruct((toks, inner), F32),
            jax.ShapeDtypeStruct((count, states, inner), BF16),
        ],
        scratch_shapes=[pltpu.VMEM((states, inner), F32)],
        compiler_params=pltpu.CompilerParams(vmem_limit_bytes=48 * 2**20),
        cost_estimate=pl.CostEstimate(flops=6 * 10**9, bytes_accessed=24 * 10**6, transcendentals=4 * 10**6),
    )(*pieces)


def scan_backward(pieces, held, dy):
    u = pieces[0]
    toks, inner = u.shape
    states, heads = pieces[1].shape[1], pieces[3].shape[1]
    count = toks // CHUNK
    order = lambda i: count - 1 - i
    wide = pl.BlockSpec((CHUNK, inner), lambda i: (order(i), 0))
    state_cols = pl.BlockSpec((CHUNK, states), lambda i: (order(i), 0))
    head_cols = pl.BlockSpec((CHUNK, heads), lambda i: (order(i), 0))
    return pl.pallas_call(
        scan_back_kernel,
        grid=(count,),
        in_specs=scan_specs(count, inner, heads, states, order)
        + [pl.BlockSpec((1, states, inner), lambda i: (order(i), 0, 0)), wide],
        out_specs=[
            wide,
            state_cols,
            state_cols,
            head_cols,
            pl.BlockSpec((heads, CHUNK), lambda i: (0, order(i))),
            head_cols,
            head_cols,
            pl.BlockSpec((1, 8, heads), lambda i: (order(i), 0, 0)),
        ],
        out_shape=[
            jax.ShapeDtypeStruct((toks, inner), F32),
            jax.ShapeDtypeStruct((toks, states), F32),
            jax.ShapeDtypeStruct((toks, states), F32),
            jax.ShapeDtypeStruct((toks, heads), F32),
            jax.ShapeDtypeStruct((heads, toks), F32),
            jax.ShapeDtypeStruct((toks, heads), F32),
            jax.ShapeDtypeStruct((toks, heads), F32),
            jax.ShapeDtypeStruct((count, 8, heads), F32),
        ],
        scratch_shapes=[pltpu.VMEM((states, inner), F32)],
        compiler_params=pltpu.CompilerParams(vmem_limit_bytes=48 * 2**20),
        cost_estimate=pl.CostEstimate(flops=20 * 10**9, bytes_accessed=40 * 10**6, transcendentals=4 * 10**6),
    )(*pieces, held, dy)


def before_scan(conv_in, step_raw, conv_weight, conv_bias, step_bias, decay_log, seg_rows, inner_size):
    width_xbc = conv_weight.shape[1]
    conv_size = conv_weight.shape[0]
    state_size = (width_xbc - inner_size) // 2
    tok_count = conv_in.shape[0]
    head_count = step_bias.shape[0]
    head_size = inner_size // head_count
    count = tok_count // CHUNK
    padded = jnp.concatenate([jnp.zeros((conv_size - 1, width_xbc), F32), conv_in], 0)
    seg_pad = jnp.concatenate([jnp.full((conv_size - 1,), -1, jnp.int32), seg_rows], 0)
    conv_pre = conv_bias + conv_weight[conv_size - 1] * conv_in
    for offset in range(1, conv_size):
        begin = conv_size - 1 - offset
        earlier = padded[begin : begin + tok_count]
        same_seg = (seg_pad[begin : begin + tok_count] == seg_rows).astype(F32)
        conv_pre = conv_pre + conv_weight[begin] * earlier * same_seg[:, None]
    conv_out = jax.nn.silu(conv_pre)
    head_flat = conv_out[:, :inner_size]
    input_map = conv_out[:, inner_size : inner_size + state_size]
    output_map = conv_out[:, inner_size + state_size :]
    step_size = jax.nn.softplus(step_raw + step_bias)
    log_rate = -step_size * jnp.exp(decay_log)
    lower = jnp.tril(jnp.ones((CHUNK, CHUNK), F32))
    cum = jnp.einsum(
        "ts,csh->cth", lower, log_rate.reshape(count, CHUNK, head_count), precision=lax.Precision.HIGHEST
    )
    seg_chunks = seg_rows.reshape(count, CHUNK)
    final = seg_chunks[:, -1]
    prior = jnp.concatenate([jnp.full((1,), -1, jnp.int32), final[:-1]])
    last = cum[:, -1:, :]
    entering = (seg_chunks == prior[:, None]).astype(F32)[:, :, None]
    leaving = (seg_chunks == final[:, None]).astype(F32)[:, :, None]
    d_in = (jnp.exp(cum) * entering).reshape(tok_count, head_count)
    d_out = (jnp.exp(last - cum) * leaving).reshape(tok_count, head_count)
    keep = jnp.exp(last[:, 0, :]) * (final == prior).astype(F32)[:, None]
    scaled = head_flat * jnp.repeat(step_size, head_size, axis=1)
    return scaled, input_map, output_map, cum.reshape(tok_count, head_count), d_in, d_out, keep, head_flat


def after_scan(scan_y, head_flat, gate_in, skip_gain, gate_gain):
    head_size = head_flat.shape[1] // skip_gain.shape[0]
    scan_out = scan_y + jnp.repeat(skip_gain, head_size)[None, :] * head_flat
    gated = scan_out * jax.nn.silu(gate_in)
    return gated * lax.rsqrt(jnp.mean(gated * gated, -1, keepdims=True) + epsilon) * gate_gain


def mixer_forward(gate_in, conv_in, step_raw, conv_w, conv_b, step_bias, decay_log, skip_gain, gate_gain, seg):
    inner = gate_in.shape[1]
    toks = gate_in.shape[0]
    heads = step_bias.shape[0]
    pre = lambda *vals: before_scan(*vals, seg, inner)
    (u, b, c, cum, d_in, d_out, keep, head_flat), pre_back = jax.vjp(
        pre, conv_in, step_raw, conv_w, conv_b, step_bias, decay_log
    )
    table = jnp.repeat(jnp.eye(heads, dtype=BF16), inner // heads, axis=1)
    keep_rows = jnp.broadcast_to(keep[:, None, :], (keep.shape[0], 8, heads))
    pieces = (u, b, c, cum, cum.T, d_in, d_out, keep_rows, seg.reshape(toks, 1), seg.reshape(1, toks), table)
    scan_y, held = scan_forward(pieces)
    gated, post_back = jax.vjp(after_scan, scan_y, head_flat, gate_in, skip_gain, gate_gain)

    def scan_back(dy, dhead):
        du, db, dc, drow, dcol, ddin, ddout, dkeep = scan_backward(pieces, held, dy)
        return pre_back((du, db, dc, drow - dcol.T, ddin, ddout, dkeep[:, 0, :], dhead))

    return gated, post_back, scan_back


def rms_rows(values, gain):
    return values * lax.rsqrt(jnp.mean(values * values, -1, keepdims=True) + epsilon) * gain


def bit_steps(first_axis):
    fs = lax.axis_size("fsdp").bit_length() - 1
    rp = lax.axis_size("rep").bit_length() - 1
    reps = [("rep", bit) for bit in reversed(range(rp))]
    rest = [("fsdp", bit) for bit in range(1, fs)]
    if first_axis == "rep":
        return [("fsdp", 0)] + reps + rest
    return [("fsdp", 0)] + rest[:1] + reps + rest[1:]


def partner_list(axis, bit):
    return [(i, i ^ (1 << bit)) for i in range(lax.axis_size(axis))]


def halving_sum(values, first_axis):
    sizes = {"fsdp": lax.axis_size("fsdp").bit_length() - 1, "rep": lax.axis_size("rep").bit_length() - 1}
    dims = [("fsdp", bit) for bit in reversed(range(sizes["fsdp"]))]
    dims += [("rep", bit) for bit in reversed(range(sizes["rep"]))]
    rows = values.shape[0] >> len(dims)
    values = values.reshape((2,) * len(dims) + (rows, values.shape[1]))
    for axis, bit in bit_steps(first_axis):
        at = dims.index((axis, bit))
        mine = (lax.axis_index(axis) >> bit) & 1
        sent = lax.dynamic_index_in_dim(values, 1 - mine, at, keepdims=False).astype(BF16)
        kept = lax.dynamic_index_in_dim(values, mine, at, keepdims=False)
        values = kept + lax.ppermute(sent, axis, partner_list(axis, bit)).astype(F32)
        dims.pop(at)
    return values


def butterfly_sum(values):
    for axis, bit in bit_steps("rep"):
        values = values + lax.ppermute(values, axis, partner_list(axis, bit))
    return values


def local(
    tokens, segment_ids, in_weight, out_weight, conv_weight, conv_bias, norm_gain, gate_gain,
    step_bias, decay_log, skip_gain, cotangent,
):
    axes = ("fsdp", "rep")
    devices = lax.axis_size("fsdp") * lax.axis_size("rep")
    me = lax.axis_index("fsdp") * lax.axis_size("rep") + lax.axis_index("rep")
    rows, width = in_weight.shape
    spare = -width % 128
    smalls = [conv_weight.reshape(-1), conv_bias, norm_gain, gate_gain]
    cuts = [s.shape[0] for s in smalls]
    flat = jnp.concatenate(smalls)
    flat = jnp.pad(flat, (0, rows * spare - flat.shape[0])).reshape(rows, spare)
    in_full = lax.all_gather(jnp.concatenate([in_weight, flat], 1), axes, axis=0, tiled=True)
    out_t = lax.all_gather(out_weight.T, axes, axis=0, tiled=True)
    inner = gate_gain.shape[0] * devices
    taps, chans = conv_weight.shape
    xbc = chans * devices
    flat_all = in_full[:, width:].reshape(devices, rows * spare).astype(F32)
    ends = [sum(cuts[: i + 1]) for i in range(4)]
    conv_full = flat_all[:, : ends[0]].reshape(devices, taps, chans).transpose(1, 0, 2).reshape(taps, xbc)
    bias_full = flat_all[:, ends[0] : ends[1]].reshape(-1)
    norm_full = flat_all[:, ends[1] : ends[2]].reshape(-1)
    gate_full = flat_all[:, ends[2] : ends[3]].reshape(-1)

    hidden_in = tokens.astype(F32)
    normed, norm_pullback = jax.vjp(rms_rows, hidden_in, norm_full)
    normed_low = normed.astype(BF16)
    gate_w, conv_w = in_full[:, :inner], in_full[:, inner:]
    gate_in = jnp.dot(normed_low, gate_w, preferred_element_type=F32)
    rest = jnp.dot(normed_low, conv_w, preferred_element_type=F32)
    gated, post_back, scan_back = mixer_forward(
        gate_in, rest[:, :xbc], rest[:, xbc : width - inner], conv_full, bias_full,
        step_bias, decay_log, skip_gain, gate_full, segment_ids,
    )
    gated_low = gated.astype(BF16)
    grad_gated = jnp.dot(cotangent, out_t, preferred_element_type=F32)
    dy, dhead, dgate, grad_skip, grad_gate = post_back(grad_gated)
    contract_tok = (((0,), (0,)), ((), ()))
    dgate_low = dgate.astype(BF16)
    grad_w_out = lax.dot_general(cotangent, gated_low, contract_tok, preferred_element_type=F32)
    grad_w_gate = lax.dot_general(normed_low, dgate_low, contract_tok, preferred_element_type=F32)
    share_out = halving_sum(grad_w_out, "fsdp")
    share_gate = halving_sum(grad_w_gate, "rep")
    branch = lax.dot_general(gated_low, out_t, (((1,), (1,)), ((), ())), preferred_element_type=F32)
    mixed = (hidden_in + branch).astype(BF16)

    dconv, dstep, grad_conv_w, grad_conv_b, grad_step, grad_decay = scan_back(dy, dhead)
    drest = jnp.concatenate([dconv, dstep], 1).astype(BF16)
    drest = jnp.pad(drest, ((0, 0), (0, spare)))
    half = xbc // 256 * 128
    share_a = halving_sum(
        lax.dot_general(normed_low, drest[:, :half], contract_tok, preferred_element_type=F32), "rep"
    )
    share_b = halving_sum(
        lax.dot_general(normed_low, drest[:, half:], contract_tok, preferred_element_type=F32), "fsdp"
    )
    contract_col = (((1,), (1,)), ((), ()))
    grad_normed = lax.dot_general(dgate_low, gate_w, contract_col, preferred_element_type=F32)
    grad_normed = grad_normed + lax.dot_general(drest, conv_w, contract_col, preferred_element_type=F32)
    grad_hidden, grad_norm = norm_pullback(grad_normed)
    grad_tokens = (cotangent.astype(F32) + grad_hidden).astype(BF16)
    flat_grads = [grad_conv_w.reshape(-1), grad_conv_b, grad_norm, grad_gate, grad_step, grad_decay, grad_skip]
    sizes = [g.shape[0] for g in flat_grads]
    total = butterfly_sum(jnp.concatenate(flat_grads))
    starts = [sum(sizes[:i]) for i in range(len(sizes))]
    sums = [total[s : s + n] for s, n in zip(starts, sizes)]
    mine = lambda vec, n: lax.dynamic_slice_in_dim(vec, me * n, n, vec.ndim - 1)
    share_in = jnp.concatenate([share_gate, share_a, share_b], 1)[:, :width]
    return (
        mixed,
        grad_tokens,
        share_in,
        share_out.T,
        mine(sums[0].reshape(taps, xbc), chans),
        mine(sums[1], chans),
        mine(sums[2], norm_gain.shape[0]),
        mine(sums[3], gate_gain.shape[0]),
        sums[4],
        sums[5],
        sums[6],
    )


def solution(mesh):
    in_specs = (
        P(("fsdp", "rep"), None),
        P(("fsdp", "rep")),
        P(("fsdp", "rep"), None),
        P(None, ("fsdp", "rep")),
        P(None, ("fsdp", "rep")),
        P(("fsdp", "rep")),
        P(("fsdp", "rep")),
        P(("fsdp", "rep")),
        P(),
        P(),
        P(),
        P(("fsdp", "rep"), None),
    )
    out_specs = (
        P(("fsdp", "rep"), None),
        P(("fsdp", "rep"), None),
        P(("fsdp", "rep"), None),
        P(None, ("fsdp", "rep")),
        P(None, ("fsdp", "rep")),
        P(("fsdp", "rep")),
        P(("fsdp", "rep")),
        P(("fsdp", "rep")),
        P(),
        P(),
        P(),
    )
    return jax.shard_map(local, mesh=mesh, in_specs=in_specs, out_specs=out_specs, check_vma=False)
```

time: 1700 us -> 541 us (0.32)
  local copies, waits for them, and re-layouts: 644 us -> 65.5 us
  matrix products: 343 us -> 94.2 us
  waiting for transfers between devices: 312 us -> 137 us
  blocking collectives: 150 us -> 0 us
  other arithmetic: 201 us -> 147 us
  Pallas kernels: 0 us -> 45.6 us
  starting transfers between devices: 0.15 us -> 25.8 us
  loops' own time: 20.3 us -> 0 us
    dynamic_update_slice x36 -> x0, local copies, waits for them, and re-layouts: 456 us -> none  [span_scan(): unused, outputs = lax.scan(jax.checkpoint(span_step), start_state, pieces)]
    reduce_scatter x2 -> x0, waiting for transfers between devices: 310 us -> none  [the longest x1 310 us: local(): lax.psum_scatter(grad_in_w, ('fsdp', 'rep'), scatter_dimension=0, tiled=T...]
    dot_general x62 -> x12, matrix products: 343 us -> 94.2 us  [the longest x1 14.9 us: local(): gate_in = jnp.dot(normed_low, gate_w, preferred_element_type=F32)]
    unnamed x2 -> x0, blocking collectives: 83.1 us -> none
    all_gather x2, waiting for transfers between devices: 0.02 us -> 73.5 us  [the longest x1 73.5 us: local(): lax.all_gather(jnp.concatenate([in_weight, flat], 1), axes, axis=0, tiled...]
    all_gather x1 -> x0, blocking collectives: 67.2 us -> none  [local(): lax.all_gather(conv_weight, ('fsdp', 'rep'), axis=1, tiled=True)]
    ppermute x0 -> x25, waiting for transfers between devices: none -> 62.3 us  [the longest x20 59.4 us: halving_sum(): lax.ppermute(sent, axis, partner_list(axis, bit)).astype(F32)]
    pallas_call x0 -> x2, Pallas kernels: none -> 45.6 us  [the longest x1 30.6 us: scan_backward(): pl.pallas_call(scan_back_kernel, grid=(count,), in_specs=scan_specs(count...]
  transfers between devices with their start and end apart: 4 -> 27, of which waited for: 1 -> 15; matrix products, arithmetic and copies ran while one was open for 69% -> 27% of each run, Pallas kernels for 0% -> 3%
where the time goes in v1:
time: 541 us; the launch traced here: 531 us
  other arithmetic  147 us (27%)
  waiting for transfers between devices  137 us (25%)
  matrix products  94.2 us (17%)
  local copies, waits for them, and re-layouts  65.5 us (12%)
  Pallas kernels  45.6 us (8%)
  starting transfers between devices  25.8 us (5%)
  between operations  15.7 us (3%)
    all_gather x1, waiting for transfers between devices, local(): lax.all_gather(jnp.concatenate([in_weight, flat], 1), axes, axis=0, tiled...  73.5 us
    ppermute x20, waiting for transfers between devices, halving_sum(): lax.ppermute(sent, axis, partner_list(axis, bit)).astype(F32)  59.4 us
    pallas_call x1, Pallas kernels, scan_backward(): pl.pallas_call(scan_back_kernel, grid=(count,), in_specs=scan_specs(count...  30.6 us
    mul x1, other arithmetic, before_scan(): conv_out = jax.nn.silu(conv_pre)  23 us
    reduce_sum x1, other arithmetic, before_scan(): conv_pre = conv_pre + conv_weight[begin] * earlier * same_seg[:, None]  23 us
    ppermute x20, starting transfers between devices, halving_sum(): lax.ppermute(sent, axis, partner_list(axis, bit)).astype(F32)  20 us
    reduce_sum x2, other arithmetic, after_scan(): scan_out = scan_y + jnp.repeat(skip_gain, head_size)[None, :] * head_flat  19.6 us
    add_any x1, other arithmetic, before_scan(): scaled = head_flat * jnp.repeat(step_size, head_size, axis=1)  18.7 us
  transfers between devices with their start and end apart: 27, of which 15 were waited for; matrix products, arithmetic and copies ran while one was open for 27% of the time, Pallas kernels for 3%

profile of v1, /device:TPU:0, one launch (start us, length us, event | category | flops | bytes accessed | tf_op | source)
XLA Modules:
  0.0 530.5 jit_solution(475351489492490033)
XLA Ops:
  21.5 73.5 %all-gather.3.cloned.1.call-done = bf16[1024,4480]{1,0:T(8,128)(2,1)} async-done(((bf16[32,4480]{1,0:T(8,128)(2,1)}), bf16[1024,4480]{1,0:T(8,128)(2,1)}) %all-gather.3.cloned.1.call-update) | async-done | bytes 9175056 | tf_op jit(solution)/shard_map/all_gather | solution.py:327
  99.6 7.8 %fusion.16 = f32[1024,2432]{1,0:T(8,128)S(1)} fusion(bf16[1024,4480]{1,0:T(8,128)(2,1)} %all-gather.3.cloned.1.call-done, bf16[1024,1024]{1,0:T(8,128)(2,1)S(1)} %copy-done.16, f32[1024]{0:T(1024)S(1)} %mul.401, f32[1024]{0:T(1024)S(1)} %fusion.102), kind=kOutput, calls=%fused_computation.50 | convolution fusion | flops 5104467968 | bytes 17047552 | tf_op jit(solution)/shard_map/dot_general | solution.py:344
  107.4 4.7 slice.164
  114.6 4.3 broadcast_in_dim.22
  118.9 9.2 %copy.115 = f32[1024,2048]{1,0:T(8,128)} copy(f32[1024,2048]{0,1:T(8,128)} %bitcast.171) | data formatting | bytes 16777216 | tf_op jit(solution)/shard_map/jvp()/reshape | solution.py:242
  129.8 23.0 %fusion.6 = (f32[1024,2304]{1,0:T(8,128)S(1)}, f32[1024,2304]{1,0:T(8,128)}) fusion(f32[1024]{0:T(1024)S(1)} %get-tuple-element.76, f32[2304]{0:T(1024)S(1)} %mul.415, f32[1024]{0:T(1024)S(1)} %get-tuple-element.77, f32[2304]{0:T(1024)S(1)} %mul.410, f32[1024]{0:T(1024)S(1)} %get-tuple-element.75, f32[1024,2304]{1,0:T(8,128)} %slice.164, f32[2304]{0:T(1024)S(1)} %mul.405, ...), kind=kLoop, calls=%fused_computation.17 | loop fusion | flops 35389440 | bytes 28369920 | tf_op jit(solution)/shard_map/jvp(jit(silu))/mul | solution.py:223
  156.8 12.0 %slice_multiply_fusion.1.u_ref = f32[1024,2048]{1,0:T(8,128)} fusion(f32[1024,2048]{1,0:T(8,128)} %copy.115, f32[1024,2304]{1,0:T(8,128)} %copy-done.13), kind=kLoop, calls=%fused_computation.43 | loop fusion | flops 2097152 | bytes 25165824 | tf_op jit(solution)/shard_map/jvp()/mul | solution.py:242
  168.8 15.0 %shard_map.203 = (f32[1024,2048]{1,0:T(8,128)}, bf16[8,128,2048]{2,1,0:T(8,128)(2,1)}) custom-call(f32[1024,2048]{1,0:T(8,128)} %slice_multiply_fusion.1.u_ref, f32[1024,128]{1,0:T(8,128)S(1)} %get-tuple-element.60.b_ref, f32[1024,128]{1,0:T(8,128)S(1)} %get-tuple-element.59.c_ref, f32[1024,32]{1,0:T(8,128)S(1)} %bitcast.154, f32[32,1024]{1,0:T(8,128)S(1)} %bitcast.169, ...), custom_call_target="tpu_custom_call" | custom-call | flops 6000000000 | bytes 24000000 | tf_op jit(solution)/shard_map/pallas_call | solution.py:149
  183.9 14.9 %multiply_reduce_fusion.7 = (f32[1024]{0:T(1024)S(1)}, f32[1024,2048]{1,0:T(8,128)}, f32[1024,2048]{1,0:T(8,128)}) fusion(f32[1024,2048]{1,0:T(8,128)} %get-tuple-element.21, f32[1024,2304]{1,0:T(8,128)} %copy-done.13, f32[2048]{0:T(1024)S(1)} %mul.430, bf16[1024,4480]{1,0:T(8,128)(2,1)} %all-gather.3.cloned.1.call-done, ...), kind=kOutput, calls=%fused_computation.33 | convolution fusion | flops 4318034944 | bytes 39866368 | tf_op jit(solution)/shard_map/dot_general | solution.py:343
  198.7 10.5 %fusion.109 = f32[2048,1024]{0,1:T(8,128)} fusion(bf16[1024,1024]{1,0:T(8,128)(2,1)S(1)} %copy-done.24, f32[1024,2048]{1,0:T(8,128)} %get-tuple-element.50, f32[2048]{0:T(1024)S(1)} %mul.438, f32[1024]{0:T(1024)S(1)} %fusion.103), kind=kOutput, calls=%fused_computation.231 | convolution fusion | flops 4301258752 | bytes 18886656 | tf_op jit(solution)/shard_map/dot_general | solution.py:354
  209.3 10.9 %multiply_reduce_fusion.5 = (f32[2048]{0:T(1024)}, f32[1024]{0:T(1024)S(1)}, f32[1024,2048]{1,0:T(8,128)S(1)}) fusion(f32[1024,2048]{1,0:T(8,128)} %get-tuple-element.50, f32[1024]{0:T(1024)S(1)} %fusion.103, f32[2048]{0:T(1024)S(1)} %mul.438, bf16[1024,1024]{1,0:T(8,128)(2,1)} %param.23, bf16[1024,2048]{1,0:T(8,128)(2,1)} %all-gather.5.cloned.1.call-done), kind=kOutput, calls=%fused_computation.29 | convolution fusion | flops 4307547136 | bytes 23093248 | tf_op jit(solution)/shard_map/dot_general | solution.py:350
  220.2 19.5 %multiply_reduce_fusion.4 = (f32[2048]{0:T(1024)}, f32[1024,2048]{1,0:T(8,128)}, bf16[1024,2048]{1,0:T(8,128)(2,1)}) fusion(f32[1024,2304]{1,0:T(8,128)} %copy-done.13, f32[1024,2048]{1,0:T(8,128)} %get-tuple-element.78, f32[1024,2048]{1,0:T(8,128)} %get-tuple-element.50, f32[1024]{0:T(1024)S(1)} %multiply_multiply_fusion.6, f32[1024]{0:T(1024)S(1)} %fusion.103, ...), kind=kLoop, calls=%fused_computation.28 | loop fusion | flops 46135296 | bytes 54558720 | tf_op jit(solution)/shard_map/transpose(jvp())/reduce_sum | solution.py:248
  239.7 30.6 %shard_map.204 = (f32[1024,2048]{1,0:T(8,128)}, f32[1024,128]{1,0:T(8,128)S(1)}, f32[1024,128]{1,0:T(8,128)S(1)}, f32[1024,32]{1,0:T(8,128)S(1)}, f32[32,1024]{1...) custom-call(f32[1024,2048]{1,0:T(8,128)} %slice_multiply_fusion.1.u_ref, ...), custom_call_target="tpu_custom_call" | custom-call | flops 20000000000 | bytes 40000000 | tf_op jit(solution)/shard_map/pallas_call | solution.py:176
  272.6 18.7 %multiply_add_fusion.1 = (f32[1024,2048]{1,0:T(8,128)}, f32[1024,2048]{1,0:T(8,128)}) fusion(f32[1024,2048]{1,0:T(8,128)} %get-tuple-element.25, f32[1024,2048]{1,0:T(8,128)} %copy.115, f32[1024,2048]{1,0:T(8,128)} %get-tuple-element.45.dy_ref, f32[2048]{0:T(1024)S(1)} %copy-done.33, f32[1024,2304]{1,0:T(8,128)} %copy-done.13), kind=kLoop, calls=%fused_computation.30 | loop fusion | flops 8388608 | bytes 50339840 | tf_op jit(solution)/shard_map/transpose(jvp())/add_any | solution.py:242
  291.3 9.3 %copy.124 = f32[1024,2048]{0,1:T(8,128)} copy(f32[1024,2048]{1,0:T(8,128)} %get-tuple-element.62) | data formatting | bytes 16777216 | tf_op jit(solution)/shard_map/transpose(jvp())/mul | solution.py:242
  300.6 4.7 bitcast_reduce_fusion
  310.6 23.0 %multiply_reduce_fusion.3 = (f32[2304]{0:T(1024)S(1)}, f32[2304]{0:T(1024)S(1)}, f32[2304]{0:T(1024)S(1)}, f32[2304]{0:T(1024)S(1)}, f32[2304]{0:T(1024)S(1)}, /*index=5*/f32[1024,2304]{1,0:T(8,128)S(1)}) fusion(f32[1024,2304]{1,0:T(8,128)} %slice.164, f32[1024]{0:T(1024)} %copy-done.40, f32[1024]{0:T(1024)} %copy-done.42, f32[1024]{0:T(1024)} %copy-done.38, ...), kind=kLoop, calls=%fused_computation.15 | loop fusion | flops 54252288 | bytes 47244288 | tf_op jit(solution)/shard_map/transpose(jvp())/reduce_sum | solution.py:222
  333.6 7.4 %multiply_multiply_fusion.2 = (f32[1024,2304]{1,0:T(8,128)S(1)}, f32[1024,2304]{1,0:T(8,128)}, f32[1024,2304]{1,0:T(8,128)}) fusion(f32[1024,2304]{1,0:T(8,128)S(1)} %get-tuple-element.48, f32[1024]{0:T(1024)S(1)} %copy-done.41, f32[2304]{0:T(1024)S(1)} %mul.415, f32[1024]{0:T(1024)S(1)} %copy-done.39, f32[2304]{0:T(1024)S(1)} %copy-done.29, ...), kind=kLoop, calls=%fused_computation.21 | loop fusion | flops 14155776 | bytes 37788672 | tf_op jit(solution)/shard_map/transpose(jvp())/mul | solution.py:222
  341.0 10.7 %fusion.5 = bf16[1024,2304]{1,0:T(8,128)(2,1)} fusion(f32[1024,2304]{1,0:T(8,128)} %get-tuple-element.57, f32[1024,2304]{1,0:T(8,128)} %get-tuple-element.58, f32[1024,2304]{1,0:T(8,128)S(1)} %get-tuple-element.56, f32[1024,2304]{1,0:T(8,128)S(1)} %get-tuple-element.48, f32[2304]{0:T(1024)S(1)} %copy-done.31), kind=kLoop, calls=%fused_computation.10 | loop fusion | flops 11796480 | bytes 42476544 | tf_op jit(solution)/shard_map/convert.2
  351.8 6.6 %fusion.33 = f32[1024,1152]{1,0:T(8,128)} fusion(bf16[1024,2304]{1,0:T(8,128)(2,1)} %fusion.5, bf16[1024,1024]{1,0:T(8,128)(2,1)S(1)} %copy-done.18, f32[1024]{0:T(1024)S(1)} %copy-done.51, f32[1024]{0:T(1024)S(1)} %copy-done.53), kind=kOutput, calls=%fused_computation.73 | convolution fusion | flops 2420113408 | bytes 9183232 | tf_op jit(solution)/shard_map/dot_general | solution.py:366
  360.3 4.9 fusion.31
  365.2 7.1 %fusion.112 = f32[1024,2048]{1,0:T(8,128)} fusion(bf16[1024,2048]{1,0:T(8,128)(2,1)S(1)} %copy-done.21, bf16[1024,1024]{1,0:T(8,128)(2,1)S(1)} %copy-done.18, f32[1024]{0:T(1024)S(1)} %copy-done.51, f32[1024]{0:T(1024)S(1)} %copy-done.53), kind=kOutput, calls=%fused_computation.232 | convolution fusion | flops 4299161600 | bytes 14688256 | tf_op jit(solution)/shard_map/dot_general | solution.py:355
  372.6 8.0 %fusion.26 = f32[1024,1024]{1,0:T(8,128)S(1)} fusion(bf16[1024,2048]{1,0:T(8,128)(2,1)} %get-tuple-element.55, bf16[1024,4480]{1,0:T(8,128)(2,1)} %all-gather.3.cloned.1.call-done), kind=kOutput, calls=%fused_computation.64 | convolution fusion | flops 4294967296 | bytes 12582912 | tf_op jit(solution)/shard_map/dot_general | solution.py:372
  380.7 10.5 %fusion.19 = (f32[1024]{0:T(1024)S(1)}, f32[1024]{0:T(1024)S(1)}, f32[1024,1024]{1,0:T(8,128)}) fusion(bf16[1024,1024]{1,0:T(8,128)(2,1)S(1)} %copy-done.18, f32[1024]{0:T(1024)S(1)} %copy-done.53, f32[1024]{0:T(1024)S(1)} %copy-done.51, f32[1024,1024]{1,0:T(8,128)S(1)} %fusion.26, bf16[1024,4480]{1,0:T(8,128)(2,1)} %all-gather.3.cloned.1.call-done, ...), kind=kOutput, calls=%fused_computation.53 | convolution fusion | flops 5126092800 | bytes 20267008 | tf_op jit(solution)/shard_map/dot_general | solution.py:373
  394.5 10.4 %fusion.23 = bf16[1024,1024]{1,0:T(8,128)(2,1)} fusion(bf16[1024,1024]{1,0:T(8,128)(2,1)S(1)} %copy-done.18, bf16[1024,2048]{1,0:T(8,128)(2,1)} %all-gather.5.cloned.1.call-done, f32[1024,2048]{1,0:T(8,128)} %get-tuple-element.50, f32[2048]{0:T(1024)S(1)} %copy-done.48, f32[1024]{0:T(1024)S(1)} %copy-done.55), kind=kOutput, calls=%fused_computation.57 | convolution fusion | flops 4304404480 | bytes 16789504 | tf_op jit(solution)/shard_map/dot_general | solution.py:358
  416.6 3.9 fusion.36
  437.3 10.6 %collective-permute-done.6 = bf16[2,2,2,32,1152]{4,3,0,1,2:T(8,128)(2,1)S(1)} collective-permute-done((bf16[2,2,2,32,1152]{4,3,0,1,2:T(8,128)(2,1)S(1)}, bf16[2,2,2,32,1152]{4,3,0,1,2:T(8,128)(2,1)S(1)}, u32[]{:S(2)}, u32[]{:S(2)}) %collective-permute-start.6) | collective-permute-done | bytes 589856 | tf_op jit(solution)/shard_map/ppermute | solution.py:303
  449.1 4.9 collective-permute-done.11
  478.4 7.8 %collective-permute-done.1 = bf16[2,2,2,32,2048]{4,3,0,1,2:T(8,128)(2,1)S(1)} collective-permute-done((bf16[2,2,2,32,2048]{4,3,0,1,2:T(8,128)(2,1)S(1)}, bf16[2,2,2,32,2048]{4,3,0,1,2:T(8,128)(2,1)S(1)}, u32[]{:S(2)}, u32[]{:S(2)}) %collective-permute-start.1) | collective-permute-done | bytes 1048608 | tf_op jit(solution)/shard_map/ppermute | solution.py:303
  487.5 4.6 collective-permute-done.16
  493.5 7.4 %collective-permute-done.2 = bf16[2,2,32,2048]{3,2,0,1:T(8,128)(2,1)S(1)} collective-permute-done((bf16[2,2,32,2048]{3,2,0,1:T(8,128)(2,1)S(1)}, bf16[2,2,32,2048]{3,2,0,1:T(8,128)(2,1)S(1)}, u32[]{:S(2)}, u32[]{:S(2)}) %collective-permute-start.2) | collective-permute-done | bytes 524320 | tf_op jit(solution)/shard_map/ppermute | solution.py:303
  503.7 7.5 %collective-permute-done.3 = bf16[2,32,2048]{2,1,0:T(8,128)(2,1)S(1)} collective-permute-done((bf16[2,32,2048]{2,1,0:T(8,128)(2,1)S(1)}, bf16[2,32,2048]{2,1,0:T(8,128)(2,1)S(1)}, u32[]{:S(2)}, u32[]{:S(2)}) %collective-permute-start.3) | collective-permute-done | bytes 262176 | tf_op jit(solution)/shard_map/ppermute | solution.py:303
  (312 shorter events, 111.0 us)
Async XLA Ops:
  7.2 87.8 %all-gather.3.cloned.1.call-start = ((), (), s32[]{:S(2)}) async-start(), calls=%async_computation | async-start | bytes 9461760 | tf_op jit(solution)/shard_map/all_gather | solution.py:327
  10.8 198.5 %all-gather.5.cloned.1.call-start = ((), (), s32[]{:S(2)}) async-start(), calls=%async_computation.1 | async-start | bytes 4325376 | tf_op jit(solution)/shard_map/all_gather | solution.py:328
  17.0 166.8 %copy-start.52 = (f32[1024]{0:T(1024)}, f32[1024]{0:T(1024)S(1)}, u32[]{:S(2)}) copy-start(f32[1024]{0:T(1024)S(1)} %fusion.102) | copy-start | bytes 12292
  18.5 150.3 %copy-start.4 = (s32[1024,1]{1,0:T(8,128)}, s32[1024,1]{1,0:T(8,128)S(1)}, u32[]{:S(2)}) copy-start(s32[1024,1]{1,0:T(8,128)S(1)} %copy.120.segc_ref) | copy-start | bytes 12292
  19.7 200.4 %copy-start.32 = (f32[2048]{0:T(1024)}, f32[2048]{0:T(1024)S(1)}, u32[]{:S(2)}) copy-start(f32[2048]{0:T(1024)S(1)} %mul.430) | copy-start | bytes 24580
  20.6 132.3 %copy-start.36 = (f32[8,128]{1,0:T(8,128)}, f32[8,128]{1,0:T(8,128)S(1)}, u32[]{:S(2)}) copy-start(f32[8,128]{1,0:T(8,128)S(1)} %get-tuple-element.73) | copy-start | bytes 12292
  20.6 132.3 %copy-start.44 = (f32[8,128]{1,0:T(8,128)}, f32[8,128]{1,0:T(8,128)S(1)}, u32[]{:S(2)}) copy-start(f32[8,128]{1,0:T(8,128)S(1)} %get-tuple-element.74) | copy-start | bytes 12292
  391.3 14.0 %collective-permute-start.20 = (f32[14688]{0:T(1024)S(1)}, f32[14688]{0:T(1024)S(1)}, u32[]{:S(2)}, u32[]{:S(2)}) collective-permute-start(f32[14688]{0:T(1024)S(1)} %concatenate.36), channel_id=1, source_target_pairs={{0,2},{2,0},{4,6},{6,4},{8,10},{10,8},{12,14},{14,12},{16,18},{18,... | collective-permute-start | bytes 176264 | tf_op jit(solution)/shard_map/ppermute | solution.py:310
  404.9 28.7 %collective-permute-start.10 = (bf16[2,2,2,2,32,1280]{5,4,0,1,3,2:T(8,128)(2,1)}, bf16[2,2,2,2,32,1280]{5,4,0,1,3,2:T(8,128)(2,1)}, u32[]{:S(2)}, u32[]{:S(2)}) collective-permute-start(bf16[2,2,2,2,32,1280]{5,4,0,1,3,2:T(8,128)(2,1)} %fusion.40), channel_id=1, source_target_pairs={{0,2},{2,0},{4,6},{6,4},{8,10},{10,8},{12,14},{14,12},{16,18},{18,... | collective-permute-start | bytes 3932168 | tf_op jit(solution)/shard_map/ppermute | solution.py:303
  405.3 4.4 collective-permute-start.21
  409.7 20.5 %collective-permute-start.5 = (bf16[2,2,2,2,32,1152]{5,4,0,1,2,3:T(8,128)(2,1)}, bf16[2,2,2,2,32,1152]{5,4,0,1,2,3:T(8,128)(2,1)}, u32[]{:S(2)}, u32[]{:S(2)}) collective-permute-start(bf16[2,2,2,2,32,1152]{5,4,0,1,2,3:T(8,128)(2,1)} %fusion.41), channel_id=1, source_target_pairs={{0,2},{2,0},{4,6},{6,4},{8,10},{10,8},{12,14},{14,12},{16,18},{18,... | collective-permute-start | bytes 3538952 | tf_op jit(solution)/shard_map/ppermute | solution.py:303
  409.8 5.2 collective-permute-start.22
  415.0 44.3 %collective-permute-start = (bf16[2,2,2,2,32,2048]{5,4,0,1,2,3:T(8,128)(2,1)}, bf16[2,2,2,2,32,2048]{5,4,0,1,2,3:T(8,128)(2,1)}, u32[]{:S(2)}, u32[]{:S(2)}) collective-permute-start(bf16[2,2,2,2,32,2048]{5,4,0,1,2,3:T(8,128)(2,1)} %fusion.35), channel_id=1, source_target_pairs={{0,2},{2,0},{4,6},{6,4},{8,10},{10,8},{12,14},{14,12},{16,18},{18,... | collective-permute-start | bytes 6291464 | tf_op jit(solution)/shard_map/ppermute | solution.py:303
  415.0 5.7 %collective-permute-start.23 = (f32[14688]{0:T(1024)S(1)}, f32[14688]{0:T(1024)S(1)}, u32[]{:S(2)}, u32[]{:S(2)}) collective-permute-start(f32[14688]{0:T(1024)S(1)} %add.319), channel_id=1, source_target_pairs={{0,8},{2,10},{4,12},{6,14},{8,0},{10,2},{12,4},{14,6},{16,24},{18,... | collective-permute-start | bytes 176264 | tf_op jit(solution)/shard_map/ppermute | solution.py:310
  420.4 42.8 %collective-permute-start.15 = (bf16[2,2,2,2,32,2048]{5,4,0,1,3,2:T(8,128)(2,1)}, bf16[2,2,2,2,32,2048]{5,4,0,1,3,2:T(8,128)(2,1)}, u32[]{:S(2)}, u32[]{:S(2)}) collective-permute-start(bf16[2,2,2,2,32,2048]{5,4,0,1,3,2:T(8,128)(2,1)} %fusion.36), channel_id=1, source_target_pairs={{0,2},{2,0},{4,6},{6,4},{8,10},{10,8},{12,14},{14,12},{16,18},{18,... | collective-permute-start | bytes 6291464 | tf_op jit(solution)/shard_map/ppermute | solution.py:303
  420.7 6.4 %collective-permute-start.24 = (f32[14688]{0:T(1024)S(1)}, f32[14688]{0:T(1024)S(1)}, u32[]{:S(2)}, u32[]{:S(2)}) collective-permute-start(f32[14688]{0:T(1024)S(1)} %add.320), channel_id=1, source_target_pairs={{0,16},{2,18},{4,20},{6,22},{8,24},{10,26},{12,28},{14,30},{16,0},... | collective-permute-start | bytes 176264 | tf_op jit(solution)/shard_map/ppermute | solution.py:310
  432.6 15.3 %collective-permute-start.6 = (bf16[2,2,2,32,1152]{4,3,0,1,2:T(8,128)(2,1)S(1)}, bf16[2,2,2,32,1152]{4,3,0,1,2:T(8,128)(2,1)S(1)}, u32[]{:S(2)}, u32[]{:S(2)}) collective-permute-start(bf16[2,2,2,32,1152]{4,3,0,1,2:T(8,128)(2,1)S(1)} %fusion.45), channel_id=1, source_target_pairs={{0,1},{1,0},{2,3},{3,2},{4,5},{5,4},{6,7},{7,6},{8,9},{9,8},{10,11... | collective-permute-start | bytes 1769480 | tf_op jit(solution)/shard_map/ppermute | solution.py:303
  436.3 17.7 %collective-permute-start.11 = (bf16[2,2,2,32,1280]{4,3,0,1,2:T(8,128)(2,1)S(1)}, bf16[2,2,2,32,1280]{4,3,0,1,2:T(8,128)(2,1)S(1)}, u32[]{:S(2)}, u32[]{:S(2)}) collective-permute-start(bf16[2,2,2,32,1280]{4,3,0,1,2:T(8,128)(2,1)S(1)} %fusion.44), channel_id=1, source_target_pairs={{0,4},{2,6},{4,0},{6,2},{8,12},{10,14},{12,8},{14,10},{16,20},{18,... | collective-permute-start | bytes 1966088 | tf_op jit(solution)/shard_map/ppermute | solution.py:303
  448.1 11.0 %collective-permute-start.7 = (bf16[2,2,32,1152]{3,2,0,1:T(8,128)(2,1)S(1)}, bf16[2,2,32,1152]{3,2,0,1:T(8,128)(2,1)S(1)}, u32[]{:S(2)}, u32[]{:S(2)}) collective-permute-start(bf16[2,2,32,1152]{3,2,0,1:T(8,128)(2,1)S(1)} %fusion.66), channel_id=1, source_target_pairs={{0,4},{2,6},{4,0},{6,2},{8,12},{10,14},{12,8},{14,10},{16,20},{18,... | collective-permute-start | bytes 884744 | tf_op jit(solution)/shard_map/ppermute | solution.py:303
  454.2 12.7 %collective-permute-start.12 = (bf16[2,2,32,1280]{3,2,0,1:T(8,128)(2,1)S(1)}, bf16[2,2,32,1280]{3,2,0,1:T(8,128)(2,1)S(1)}, u32[]{:S(2)}, u32[]{:S(2)}) collective-permute-start(bf16[2,2,32,1280]{3,2,0,1:T(8,128)(2,1)S(1)} %fusion.65), channel_id=1, source_target_pairs={{0,1},{1,0},{2,3},{3,2},{4,5},{5,4},{6,7},{7,6},{8,9},{9,8},{10,11... | collective-permute-start | bytes 983048 | tf_op jit(solution)/shard_map/ppermute | solution.py:303
  459.2 7.7 %collective-permute-start.8 = (bf16[2,32,1152]{2,1,0:T(8,128)(2,1)S(1)}, bf16[2,32,1152]{2,1,0:T(8,128)(2,1)S(1)}, u32[]{:S(2)}, u32[]{:S(2)}) collective-permute-start(bf16[2,32,1152]{2,1,0:T(8,128)(2,1)S(1)} %fusion.74), channel_id=1, source_target_pairs={{0,8},{2,10},{4,12},{6,14},{8,0},{10,2},{12,4},{14,6},{16,24},{18,... | collective-permute-start | bytes 442376 | tf_op jit(solution)/shard_map/ppermute | solution.py:303
  462.2 24.0 %collective-permute-start.1 = (bf16[2,2,2,32,2048]{4,3,0,1,2:T(8,128)(2,1)S(1)}, bf16[2,2,2,32,2048]{4,3,0,1,2:T(8,128)(2,1)S(1)}, u32[]{:S(2)}, u32[]{:S(2)}) collective-permute-start(bf16[2,2,2,32,2048]{4,3,0,1,2:T(8,128)(2,1)S(1)} %fusion.42), channel_id=1, source_target_pairs={{0,1},{1,0},{2,3},{3,2},{4,5},{5,4},{6,7},{7,6},{8,9},{9,8},{10,11... | collective-permute-start | bytes 3145736 | tf_op jit(solution)/shard_map/ppermute | solution.py:303
  465.9 26.2 %collective-permute-start.16 = (bf16[2,2,2,32,2048]{4,3,0,1,2:T(8,128)(2,1)S(1)}, bf16[2,2,2,32,2048]{4,3,0,1,2:T(8,128)(2,1)S(1)}, u32[]{:S(2)}, u32[]{:S(2)}) collective-permute-start(bf16[2,2,2,32,2048]{4,3,0,1,2:T(8,128)(2,1)S(1)} %fusion.43), channel_id=1, source_target_pairs={{0,4},{2,6},{4,0},{6,2},{8,12},{10,14},{12,8},{14,10},{16,20},{18,... | collective-permute-start | bytes 3145736 | tf_op jit(solution)/shard_map/ppermute | solution.py:303
  467.0 5.8 %collective-permute-start.13 = (bf16[2,32,1280]{2,1,0:T(8,128)(2,1)S(1)}, bf16[2,32,1280]{2,1,0:T(8,128)(2,1)S(1)}, u32[]{:S(2)}, u32[]{:S(2)}) collective-permute-start(bf16[2,32,1280]{2,1,0:T(8,128)(2,1)S(1)} %fusion.73), channel_id=1, source_target_pairs={{0,8},{2,10},{4,12},{6,14},{8,0},{10,2},{12,4},{14,6},{16,24},{18,... | collective-permute-start | bytes 491528 | tf_op jit(solution)/shard_map/ppermute | solution.py:303
  469.0 7.7 %collective-permute-start.9 = (bf16[32,1152]{1,0:T(8,128)(2,1)S(1)}, bf16[32,1152]{1,0:T(8,128)(2,1)S(1)}, u32[]{:S(2)}, u32[]{:S(2)}) collective-permute-start(bf16[32,1152]{1,0:T(8,128)(2,1)S(1)} %fusion.78), channel_id=1, source_target_pairs={{0,16},{2,18},{4,20},{6,22},{8,24},{10,26},{12,28},{14,30},{16,0},... | collective-permute-start | bytes 221192 | tf_op jit(solution)/shard_map/ppermute | solution.py:303
  472.9 5.4 %collective-permute-start.14 = (bf16[32,1280]{1,0:T(8,128)(2,1)S(1)}, bf16[32,1280]{1,0:T(8,128)(2,1)S(1)}, u32[]{:S(2)}, u32[]{:S(2)}) collective-permute-start(bf16[32,1280]{1,0:T(8,128)(2,1)S(1)} %fusion.77), channel_id=1, source_target_pairs={{0,16},{2,18},{4,20},{6,22},{8,24},{10,26},{12,28},{14,30},{16,0},... | collective-permute-start | bytes 245768 | tf_op jit(solution)/shard_map/ppermute | solution.py:303
  486.5 14.3 %collective-permute-start.2 = (bf16[2,2,32,2048]{3,2,0,1:T(8,128)(2,1)S(1)}, bf16[2,2,32,2048]{3,2,0,1:T(8,128)(2,1)S(1)}, u32[]{:S(2)}, u32[]{:S(2)}) collective-permute-start(bf16[2,2,32,2048]{3,2,0,1:T(8,128)(2,1)S(1)} %fusion.46), channel_id=1, source_target_pairs={{0,4},{2,6},{4,0},{6,2},{8,12},{10,14},{12,8},{14,10},{16,20},{18,... | collective-permute-start | bytes 1572872 | tf_op jit(solution)/shard_map/ppermute | solution.py:303
  492.4 10.3 %collective-permute-start.17 = (bf16[2,2,32,2048]{3,2,0,1:T(8,128)(2,1)S(1)}, bf16[2,2,32,2048]{3,2,0,1:T(8,128)(2,1)S(1)}, u32[]{:S(2)}, u32[]{:S(2)}) collective-permute-start(bf16[2,2,32,2048]{3,2,0,1:T(8,128)(2,1)S(1)} %fusion.47), channel_id=1, source_target_pairs={{0,1},{1,0},{2,3},{3,2},{4,5},{5,4},{6,7},{7,6},{8,9},{9,8},{10,11... | collective-permute-start | bytes 1572872 | tf_op jit(solution)/shard_map/ppermute | solution.py:303
  501.0 10.2 %collective-permute-start.3 = (bf16[2,32,2048]{2,1,0:T(8,128)(2,1)S(1)}, bf16[2,32,2048]{2,1,0:T(8,128)(2,1)S(1)}, u32[]{:S(2)}, u32[]{:S(2)}) collective-permute-start(bf16[2,32,2048]{2,1,0:T(8,128)(2,1)S(1)} %fusion.67), channel_id=1, source_target_pairs={{0,8},{2,10},{4,12},{6,14},{8,0},{10,2},{12,4},{14,6},{16,24},{18,... | collective-permute-start | bytes 786440 | tf_op jit(solution)/shard_map/ppermute | solution.py:303
  502.9 11.4 %collective-permute-start.18 = (bf16[2,32,2048]{2,1,0:T(8,128)(2,1)S(1)}, bf16[2,32,2048]{2,1,0:T(8,128)(2,1)S(1)}, u32[]{:S(2)}, u32[]{:S(2)}) collective-permute-start(bf16[2,32,2048]{2,1,0:T(8,128)(2,1)S(1)} %fusion.68), channel_id=1, source_target_pairs={{0,8},{2,10},{4,12},{6,14},{8,0},{10,2},{12,4},{14,6},{16,24},{18,... | collective-permute-start | bytes 786440 | tf_op jit(solution)/shard_map/ppermute | solution.py:303
  511.3 8.4 %collective-permute-start.4 = (bf16[32,2048]{1,0:T(8,128)(2,1)S(1)}, bf16[32,2048]{1,0:T(8,128)(2,1)S(1)}, u32[]{:S(2)}, u32[]{:S(2)}) collective-permute-start(bf16[32,2048]{1,0:T(8,128)(2,1)S(1)} %fusion.75), channel_id=1, source_target_pairs={{0,16},{2,18},{4,20},{6,22},{8,24},{10,26},{12,28},{14,30},{16,0},... | collective-permute-start | bytes 393224 | tf_op jit(solution)/shard_map/ppermute | solution.py:303
  514.3 8.2 %collective-permute-start.19 = (bf16[32,2048]{1,0:T(8,128)(2,1)S(1)}, bf16[32,2048]{1,0:T(8,128)(2,1)S(1)}, u32[]{:S(2)}, u32[]{:S(2)}) collective-permute-start(bf16[32,2048]{1,0:T(8,128)(2,1)S(1)} %fusion.76), channel_id=1, source_target_pairs={{0,16},{2,18},{4,20},{6,22},{8,24},{10,26},{12,28},{14,30},{16,0},... | collective-permute-start | bytes 393224 | tf_op jit(solution)/shard_map/ppermute | solution.py:303
  (65 other events, 1568.8 us)
Sparse Core Ops, SparseCore 0:
  11.4 83.5 all-gather.2
  98.0 60.6 all-gather.4

commit v2 on v1

--- a/solution.py
+++ b/solution.py
@@ -33,14 +33,15 @@
 
 
 def scan_kernel(
-    u_ref, b_ref, c_ref, cum_ref, cumt_ref, din_ref, dout_ref, keep_ref, segc_ref, segr_ref, table_ref,
-    y_ref, held_ref, state_ref,
+    x_ref, b_ref, c_ref, cum_ref, cumt_ref, din_ref, dout_ref, keep_ref, segc_ref, segr_ref, table_ref, dt_ref,
+    y_ref, held_ref, state_ref, u_ref,
 ):
     @pl.when(pl.program_id(0) == 0)
     def _():
         state_ref[...] = jnp.zeros_like(state_ref)
 
     table = table_ref[...]
+    u_ref[...] = x_ref[...] * two_part(dt_ref[...], table, 0)
     b_part, c_part = b_ref[...], c_ref[...]
     mask = chunk_mask(segc_ref[...], segr_ref[...])
     scores = jnp.where(mask, dot_at(c_part, b_part, 1, 1), 0.0)
@@ -66,15 +67,17 @@
 
 
 def scan_back_kernel(
-    u_ref, b_ref, c_ref, cum_ref, cumt_ref, din_ref, dout_ref, keep_ref, segc_ref, segr_ref, table_ref,
+    x_ref, b_ref, c_ref, cum_ref, cumt_ref, din_ref, dout_ref, keep_ref, segc_ref, segr_ref, table_ref, dt_ref,
     held_ref, dy_ref,
-    du_ref, db_ref, dc_ref, drow_ref, dcol_ref, ddin_ref, ddout_ref, dkeep_ref, dstate_ref,
+    dx_ref, db_ref, dc_ref, drow_ref, dcol_ref, ddin_ref, ddout_ref, dkeep_ref, ddt_ref, dstate_ref, u_ref, du_ref,
 ):
     @pl.when(pl.program_id(0) == 0)
     def _():
         dstate_ref[...] = jnp.zeros_like(dstate_ref)
 
     table = table_ref[...]
+    dt_wide = two_part(dt_ref[...], table, 0)
+    u_ref[...] = x_ref[...] * dt_wide
     b_part, c_part = b_ref[...].astype(BF16), c_ref[...].astype(BF16)
     mask = chunk_mask(segc_ref[...], segr_ref[...])
     scores = jnp.where(mask, dot_at(c_part, b_part, 1, 1), 0.0)
@@ -123,6 +126,9 @@
     dscores = jnp.where(mask, dscores, 0.0)
     dc_ref[...] = dc_carry + dot_at(dscores, b_part, 1, 0)
     db_ref[...] = db_carry + dot_at(dscores, c_part, 0, 0)
+    du_all = du_ref[...]
+    dx_ref[...] = du_all * dt_wide
+    ddt_ref[...] = two_part(du_all * x_ref[...], table, 1)
 
 
 def scan_specs(count, inner, heads, states, order):
@@ -138,6 +144,7 @@
         pl.BlockSpec((CHUNK, 1), lambda i: (order(i), 0)),
         pl.BlockSpec((1, CHUNK), lambda i: (0, order(i))),
         pl.BlockSpec((heads, inner), lambda i: (0, 0)),
+        pl.BlockSpec((CHUNK, heads), lambda i: (order(i), 0)),
     ]
 
 
@@ -158,7 +165,7 @@
             jax.ShapeDtypeStruct((toks, inner), F32),
             jax.ShapeDtypeStruct((count, states, inner), BF16),
         ],
-        scratch_shapes=[pltpu.VMEM((states, inner), F32)],
+        scratch_shapes=[pltpu.VMEM((states, inner), F32), pltpu.VMEM((CHUNK, inner), F32)],
         compiler_params=pltpu.CompilerParams(vmem_limit_bytes=48 * 2**20),
         cost_estimate=pl.CostEstimate(flops=6 * 10**9, bytes_accessed=24 * 10**6, transcendentals=4 * 10**6),
     )(*pieces)
@@ -187,6 +194,7 @@
             head_cols,
             head_cols,
             pl.BlockSpec((1, 8, heads), lambda i: (order(i), 0, 0)),
+            head_cols,
         ],
         out_shape=[
             jax.ShapeDtypeStruct((toks, inner), F32),
@@ -197,8 +205,9 @@
             jax.ShapeDtypeStruct((toks, heads), F32),
             jax.ShapeDtypeStruct((toks, heads), F32),
             jax.ShapeDtypeStruct((count, 8, heads), F32),
+            jax.ShapeDtypeStruct((toks, heads), F32),
         ],
-        scratch_shapes=[pltpu.VMEM((states, inner), F32)],
+        scratch_shapes=[pltpu.VMEM((states, inner), F32), pltpu.VMEM((CHUNK, inner), F32), pltpu.VMEM((CHUNK, inner), F32)],
         compiler_params=pltpu.CompilerParams(vmem_limit_bytes=48 * 2**20),
         cost_estimate=pl.CostEstimate(flops=20 * 10**9, bytes_accessed=40 * 10**6, transcendentals=4 * 10**6),
     )(*pieces, held, dy)
@@ -210,7 +219,6 @@
     state_size = (width_xbc - inner_size) // 2
     tok_count = conv_in.shape[0]
     head_count = step_bias.shape[0]
-    head_size = inner_size // head_count
     count = tok_count // CHUNK
     padded = jnp.concatenate([jnp.zeros((conv_size - 1, width_xbc), F32), conv_in], 0)
     seg_pad = jnp.concatenate([jnp.full((conv_size - 1,), -1, jnp.int32), seg_rows], 0)
@@ -239,8 +247,7 @@
     d_in = (jnp.exp(cum) * entering).reshape(tok_count, head_count)
     d_out = (jnp.exp(last - cum) * leaving).reshape(tok_count, head_count)
     keep = jnp.exp(last[:, 0, :]) * (final == prior).astype(F32)[:, None]
-    scaled = head_flat * jnp.repeat(step_size, head_size, axis=1)
-    return scaled, input_map, output_map, cum.reshape(tok_count, head_count), d_in, d_out, keep, head_flat
+    return head_flat, input_map, output_map, cum.reshape(tok_count, head_count), d_in, d_out, keep, step_size
 
 
 def after_scan(scan_y, head_flat, gate_in, skip_gain, gate_gain):
@@ -255,20 +262,26 @@
     toks = gate_in.shape[0]
     heads = step_bias.shape[0]
     pre = lambda *vals: before_scan(*vals, seg, inner)
-    (u, b, c, cum, d_in, d_out, keep, head_flat), pre_back = jax.vjp(
+    (head_flat, b, c, cum, d_in, d_out, keep, step_size), pre_back = jax.vjp(
         pre, conv_in, step_raw, conv_w, conv_b, step_bias, decay_log
     )
     table = jnp.repeat(jnp.eye(heads, dtype=BF16), inner // heads, axis=1)
     keep_rows = jnp.broadcast_to(keep[:, None, :], (keep.shape[0], 8, heads))
-    pieces = (u, b, c, cum, cum.T, d_in, d_out, keep_rows, seg.reshape(toks, 1), seg.reshape(1, toks), table)
+    pieces = (
+        head_flat, b, c, cum, cum.T, d_in, d_out, keep_rows,
+        seg.reshape(toks, 1), seg.reshape(1, toks), table, step_size,
+    )
     scan_y, held = scan_forward(pieces)
     gated, post_back = jax.vjp(after_scan, scan_y, head_flat, gate_in, skip_gain, gate_gain)
 
-    def scan_back(dy, dhead):
-        du, db, dc, drow, dcol, ddin, ddout, dkeep = scan_backward(pieces, held, dy)
-        return pre_back((du, db, dc, drow - dcol.T, ddin, ddout, dkeep[:, 0, :], dhead))
-
-    return gated, post_back, scan_back
+    def scan_back(dy):
+        return scan_backward(pieces, held, dy)
+
+    def before_back(grads, dhead):
+        dx, db, dc, drow, dcol, ddin, ddout, dkeep, ddt = grads
+        return pre_back((dx + dhead, db, dc, drow - dcol.T, ddin, ddout, dkeep[:, 0, :], ddt))
+
+    return gated, post_back, scan_back, before_back
 
 
 def rms_rows(values, gain):
@@ -289,20 +302,32 @@
     return [(i, i ^ (1 << bit)) for i in range(lax.axis_size(axis))]
 
 
-def halving_sum(values, first_axis):
-    sizes = {"fsdp": lax.axis_size("fsdp").bit_length() - 1, "rep": lax.axis_size("rep").bit_length() - 1}
-    dims = [("fsdp", bit) for bit in reversed(range(sizes["fsdp"]))]
-    dims += [("rep", bit) for bit in reversed(range(sizes["rep"]))]
-    rows = values.shape[0] >> len(dims)
-    values = values.reshape((2,) * len(dims) + (rows, values.shape[1]))
-    for axis, bit in bit_steps(first_axis):
-        at = dims.index((axis, bit))
+class HalvingSum:
+    def __init__(self, values, first_axis):
+        fs = lax.axis_size("fsdp").bit_length() - 1
+        rp = lax.axis_size("rep").bit_length() - 1
+        self.dims = [("fsdp", bit) for bit in reversed(range(fs))] + [("rep", bit) for bit in reversed(range(rp))]
+        rows = values.shape[0] >> len(self.dims)
+        self.values = values.reshape((2,) * len(self.dims) + (rows, values.shape[1]))
+        self.steps = bit_steps(first_axis)
+
+    def step(self, *beside):
+        axis, bit = self.steps.pop(0)
+        at = self.dims.index((axis, bit))
         mine = (lax.axis_index(axis) >> bit) & 1
-        sent = lax.dynamic_index_in_dim(values, 1 - mine, at, keepdims=False).astype(BF16)
-        kept = lax.dynamic_index_in_dim(values, mine, at, keepdims=False)
-        values = kept + lax.ppermute(sent, axis, partner_list(axis, bit)).astype(F32)
-        dims.pop(at)
-    return values
+        sent = lax.dynamic_index_in_dim(self.values, 1 - mine, at, keepdims=False).astype(BF16)
+        kept = lax.dynamic_index_in_dim(self.values, mine, at, keepdims=False)
+        got = lax.ppermute(sent, axis, partner_list(axis, bit))
+        if beside:
+            got, *beside = lax.optimization_barrier((got, *beside))
+        self.values = kept + got.astype(F32)
+        self.dims.pop(at)
+        return beside
+
+    def finish(self):
+        while self.steps:
+            self.step()
+        return self.values
 
 
 def butterfly_sum(values):
@@ -342,37 +367,46 @@
     gate_w, conv_w = in_full[:, :inner], in_full[:, inner:]
     gate_in = jnp.dot(normed_low, gate_w, preferred_element_type=F32)
     rest = jnp.dot(normed_low, conv_w, preferred_element_type=F32)
-    gated, post_back, scan_back = mixer_forward(
+    gated, post_back, scan_back, before_back = mixer_forward(
         gate_in, rest[:, :xbc], rest[:, xbc : width - inner], conv_full, bias_full,
         step_bias, decay_log, skip_gain, gate_full, segment_ids,
     )
     gated_low = gated.astype(BF16)
     grad_gated = jnp.dot(cotangent, out_t, preferred_element_type=F32)
+    contract_tok = (((0,), (0,)), ((), ()))
+    contract_col = (((1,), (1,)), ((), ()))
+    grad_w_out = lax.dot_general(cotangent, gated_low, contract_tok, preferred_element_type=F32)
+    sum_out = HalvingSum(grad_w_out, "fsdp")
     dy, dhead, dgate, grad_skip, grad_gate = post_back(grad_gated)
-    contract_tok = (((0,), (0,)), ((), ()))
     dgate_low = dgate.astype(BF16)
-    grad_w_out = lax.dot_general(cotangent, gated_low, contract_tok, preferred_element_type=F32)
+    dy, dhead, dgate_low = sum_out.step(dy, dhead, dgate_low)
     grad_w_gate = lax.dot_general(normed_low, dgate_low, contract_tok, preferred_element_type=F32)
-    share_out = halving_sum(grad_w_out, "fsdp")
-    share_gate = halving_sum(grad_w_gate, "rep")
-    branch = lax.dot_general(gated_low, out_t, (((1,), (1,)), ((), ())), preferred_element_type=F32)
+    sum_gate = HalvingSum(grad_w_gate, "rep")
+    branch = lax.dot_general(gated_low, out_t, contract_col, preferred_element_type=F32)
     mixed = (hidden_in + branch).astype(BF16)
 
-    dconv, dstep, grad_conv_w, grad_conv_b, grad_step, grad_decay = scan_back(dy, dhead)
+    scan_grads = scan_back(dy)
+    scan_grads = sum_out.step(*scan_grads)
+    scan_grads = sum_gate.step(*scan_grads)
+    dconv, dstep, grad_conv_w, grad_conv_b, grad_step, grad_decay = before_back(scan_grads, dhead)
     drest = jnp.concatenate([dconv, dstep], 1).astype(BF16)
     drest = jnp.pad(drest, ((0, 0), (0, spare)))
+    (drest,) = sum_out.step(drest)
+    (drest,) = sum_gate.step(drest)
     half = xbc // 256 * 128
-    share_a = halving_sum(
-        lax.dot_general(normed_low, drest[:, :half], contract_tok, preferred_element_type=F32), "rep"
-    )
-    share_b = halving_sum(
-        lax.dot_general(normed_low, drest[:, half:], contract_tok, preferred_element_type=F32), "fsdp"
-    )
-    contract_col = (((1,), (1,)), ((), ()))
+    grad_a = lax.dot_general(normed_low, drest[:, :half], contract_tok, preferred_element_type=F32)
+    grad_b = lax.dot_general(normed_low, drest[:, half:], contract_tok, preferred_element_type=F32)
+    grad_a, grad_b = sum_out.step(grad_a, grad_b)
+    grad_a, grad_b = sum_gate.step(grad_a, grad_b)
+    sum_a, sum_b = HalvingSum(grad_a, "rep"), HalvingSum(grad_b, "fsdp")
     grad_normed = lax.dot_general(dgate_low, gate_w, contract_col, preferred_element_type=F32)
     grad_normed = grad_normed + lax.dot_general(drest, conv_w, contract_col, preferred_element_type=F32)
+    for share in (sum_out, sum_gate, sum_a, sum_b):
+        (grad_normed,) = share.step(grad_normed)
     grad_hidden, grad_norm = norm_pullback(grad_normed)
     grad_tokens = (cotangent.astype(F32) + grad_hidden).astype(BF16)
+    share_out, share_gate = sum_out.finish(), sum_gate.finish()
+    share_a, share_b = sum_a.finish(), sum_b.finish()
     flat_grads = [grad_conv_w.reshape(-1), grad_conv_b, grad_norm, grad_gate, grad_step, grad_decay, grad_skip]
     sizes = [g.shape[0] for g in flat_grads]
     total = butterfly_sum(jnp.concatenate(flat_grads))

time: 541 us -> 512 us (0.946)
  local copies, waits for them, and re-layouts: 65.5 us -> 43.4 us
  waiting for transfers between devices: 137 us -> 128 us
  matrix products: 94.2 us -> 86.3 us
  Pallas kernels: 45.6 us -> 53.5 us
    ppermute x20, waiting for transfers between devices: 59.4 us -> 33.1 us  [step(): got = lax.ppermute(sent, axis, partner_list(axis, bit))]
    add x19 -> x20, other arithmetic: 11.4 us -> 33.9 us  [the longest x19 22.1 us: step(): self.values = kept + got.astype(F32)]
    add_any x1 -> x0, other arithmetic: 18.7 us -> none  [before_scan(): scaled = head_flat * jnp.repeat(step_size, head_size, axis=1)]
    ppermute x5, waiting for transfers between devices: 2.83 us -> 20.8 us  [butterfly_sum(): values = values + lax.ppermute(values, axis, partner_list(axis, bit))]
    mul x1 -> x0, local copies, waits for them, and re-layouts: 9.31 us -> none  [before_scan(): scaled = head_flat * jnp.repeat(step_size, head_size, axis=1)]
    reshape x1 -> x0, local copies, waits for them, and re-layouts: 9.18 us -> none  [before_scan(): scaled = head_flat * jnp.repeat(step_size, head_size, axis=1)]
    pallas_call x1, Pallas kernels: 30.6 us -> 36.8 us  [scan_backward(): pl.pallas_call(scan_back_kernel, grid=(count,), in_specs=scan_specs(count...]
  transfers between devices with their start and end apart: 27 -> 27, of which waited for: 15 -> 13; matrix products, arithmetic and copies ran while one was open for 27% -> 45% of each run, Pallas kernels for 3% -> 11%
where the time goes in v2:
time: 512 us; the launch traced here: 502 us
  other arithmetic  150 us (29%)
  waiting for transfers between devices  128 us (25%)
  matrix products  86.3 us (17%)
  Pallas kernels  53.5 us (10%)
  local copies, waits for them, and re-layouts  43.4 us (8%)
  starting transfers between devices  24.3 us (5%)
  between operations  15.8 us (3%)
    all_gather x1, waiting for transfers between devices, local(): lax.all_gather(jnp.concatenate([in_weight, flat], 1), axes, axis=0, tiled...  73.9 us
    pallas_call x1, Pallas kernels, scan_backward(): pl.pallas_call(scan_back_kernel, grid=(count,), in_specs=scan_specs(count...  36.8 us
    ppermute x20, waiting for transfers between devices, step(): got = lax.ppermute(sent, axis, partner_list(axis, bit))  33.1 us
    mul x1, other arithmetic, before_scan(): conv_out = jax.nn.silu(conv_pre)  23.1 us
    reduce_sum x1, other arithmetic, before_scan(): conv_pre = conv_pre + conv_weight[begin] * earlier * same_seg[:, None]  23 us
    add x19, other arithmetic, step(): self.values = kept + got.astype(F32)  22.1 us
    ppermute x20, starting transfers between devices, step(): got = lax.ppermute(sent, axis, partner_list(axis, bit))  21.4 us
    ppermute x5, waiting for transfers between devices, butterfly_sum(): values = values + lax.ppermute(values, axis, partner_list(axis, bit))  20.8 us
  transfers between devices with their start and end apart: 27, of which 13 were waited for; matrix products, arithmetic and copies ran while one was open for 45% of the time, Pallas kernels for 11%

profile of v2, /device:TPU:0, one launch (start us, length us, event | category | flops | bytes accessed | tf_op | source)
XLA Modules:
  0.0 501.9 jit_solution(11630320451031639910)
XLA Ops:
  20.9 73.9 %all-gather.3.cloned.1.call-done = bf16[1024,4480]{1,0:T(8,128)(2,1)} async-done(((bf16[32,4480]{1,0:T(8,128)(2,1)}), bf16[1024,4480]{1,0:T(8,128)(2,1)}) %all-gather.3.cloned.1.call-update) | async-done | bytes 9175056 | tf_op jit(solution)/shard_map/all_gather | solution.py:352
  100.5 7.9 %fusion.16 = f32[1024,2432]{1,0:T(8,128)S(1)} fusion(bf16[1024,4480]{1,0:T(8,128)(2,1)} %all-gather.3.cloned.1.call-done, bf16[1024,1024]{1,0:T(8,128)(2,1)S(1)} %copy-done.17, f32[1024]{0:T(1024)S(1)} %mul.392, f32[1024]{0:T(1024)S(1)} %fusion.102), kind=kOutput, calls=%fused_computation.46 | convolution fusion | flops 5104467968 | bytes 17047552 | tf_op jit(solution)/shard_map/dot_general | solution.py:369
  108.4 4.7 slice.162
  116.7 23.1 %fusion.6 = (f32[1024,2304]{1,0:T(8,128)S(1)}, f32[1024,2304]{1,0:T(8,128)}) fusion(f32[1024]{0:T(1024)S(1)} %get-tuple-element.160, f32[2304]{0:T(1024)S(1)} %mul.406, f32[1024]{0:T(1024)S(1)} %get-tuple-element.161, f32[2304]{0:T(1024)S(1)} %mul.401, f32[1024]{0:T(1024)S(1)} %get-tuple-element.159, f32[1024,2304]{1,0:T(8,128)} %slice.162, ...), kind=kLoop, calls=%fused_computation.17 | loop fusion | flops 35389440 | bytes 28369920 | tf_op jit(solution)/shard_map/jvp(jit(silu))/mul | solution.py:231
  139.8 4.9 slice.166.x_ref
  146.5 16.7 %shard_map.203 = (f32[1024,2048]{1,0:T(8,128)}, bf16[8,128,2048]{2,1,0:T(8,128)(2,1)}) custom-call(f32[1024,2048]{1,0:T(8,128)} %slice.166.x_ref, f32[1024,128]{1,0:T(8,128)S(1)} %get-tuple-element.146.b_ref, f32[1024,128]{1,0:T(8,128)S(1)} %get-tuple-element.145.c_ref, f32[1024,32]{1,0:T(8,128)S(1)} %bitcast.152, f32[32,1024]{1,0:T(8,128)S(1)} %bitcast.167, ...), custom_call_target="tpu_custom_call" | custom-call | flops 6000000000 | bytes 24000000 | tf_op jit(solution)/shard_map/pallas_call | solution.py:156
  163.3 14.9 %multiply_reduce_fusion.7 = (f32[1024]{0:T(1024)S(1)}, f32[1024,2048]{1,0:T(8,128)}, f32[1024,2048]{1,0:T(8,128)}) fusion(f32[1024,2048]{1,0:T(8,128)} %get-tuple-element.64, f32[1024,2304]{1,0:T(8,128)} %copy-done.15, f32[2048]{0:T(1024)S(1)} %mul.420, bf16[1024,4480]{1,0:T(8,128)(2,1)} %all-gather.3.cloned.1.call-done, ...), kind=kOutput, calls=%fused_computation.31 | convolution fusion | flops 4318034944 | bytes 39866368 | tf_op jit(solution)/shard_map/dot_general | solution.py:368
  178.2 10.6 %fusion.109 = f32[2048,1024]{0,1:T(8,128)} fusion(bf16[1024,1024]{1,0:T(8,128)(2,1)S(1)} %copy-done.30, f32[1024,2048]{1,0:T(8,128)} %get-tuple-element.136, f32[2048]{0:T(1024)S(1)} %mul.428, f32[1024]{0:T(1024)S(1)} %fusion.103), kind=kOutput, calls=%fused_computation.228 | convolution fusion | flops 4301258752 | bytes 18886656 | tf_op jit(solution)/shard_map/dot_general | solution.py:378
  188.9 11.0 %multiply_reduce_fusion.5 = (f32[2048]{0:T(1024)}, f32[1024]{0:T(1024)S(1)}, f32[1024,2048]{1,0:T(8,128)S(1)}) fusion(f32[1024,2048]{1,0:T(8,128)} %get-tuple-element.136, f32[1024]{0:T(1024)S(1)} %fusion.103, f32[2048]{0:T(1024)S(1)} %mul.428, bf16[1024,1024]{1,0:T(8,128)(2,1)} %param.23, bf16[1024,2048]{1,0:T(8,128)(2,1)} %all-gather.5.cloned.1.call-done), kind=kOutput, calls=%fused_computation.28 | convolution fusion | flops 4307547136 | bytes 23093248 | tf_op jit(solution)/shard_map/dot_general | solution.py:375
  199.9 19.1 %multiply_reduce_fusion.4 = (f32[2048]{0:T(1024)S(1)}, f32[1024,2048]{1,0:T(8,128)}, bf16[1024,2048]{1,0:T(8,128)(2,1)}) fusion(f32[1024,2304]{1,0:T(8,128)} %copy-done.15, f32[1024,2048]{1,0:T(8,128)} %get-tuple-element.162, f32[1024,2048]{1,0:T(8,128)} %get-tuple-element.136, f32[1024]{0:T(1024)S(1)} %multiply_multiply_fusion.6, f32[1024]{0:T(1024)S(1)} %fusion.103, ...), kind=kLoop, calls=%fused_computation.27 | loop fusion | flops 46135296 | bytes 54558720 | tf_op jit(solution)/shard_map/transpose(jvp())/reduce_sum | solution.py:255
  219.1 3.8 fusion.35
  223.8 8.6 %broadcast_multiply_fusion = f32[1024,2048]{1,0:T(8,128)} fusion(f32[1024,2048]{1,0:T(8,128)} %get-tuple-element.68.dy_ref, f32[2048]{0:T(1024)S(1)} %mul.420), kind=kLoop, calls=%fused_computation.60 | loop fusion | flops 2097152 | bytes 16785408 | tf_op jit(solution)/shard_map/transpose(jvp())/mul | solution.py:255
  232.4 9.2 %fusion.23 = bf16[1024,1024]{1,0:T(8,128)(2,1)} fusion(bf16[1024,1024]{1,0:T(8,128)(2,1)S(1)} %copy-done.19, bf16[1024,2048]{1,0:T(8,128)(2,1)S(1)} %copy-done.65, f32[1024,2048]{1,0:T(8,128)} %get-tuple-element.136, f32[2048]{0:T(1024)S(1)} %mul.428, f32[1024]{0:T(1024)S(1)} %fusion.103), kind=kOutput, calls=%fused_computation.53 | convolution fusion | flops 4304404480 | bytes 16789504 | tf_op jit(solution)/shard_map/dot_general | solution.py:385
  241.6 3.8 bitcast_add_fusion
  247.2 4.8 fusion.112
  255.4 36.8 %shard_map.204 = (f32[1024,2048]{1,0:T(8,128)}, f32[1024,128]{1,0:T(8,128)S(1)}, f32[1024,128]{1,0:T(8,128)S(1)}, f32[1024,32]{1,0:T(8,128)S(1)}, f32[32,1024]{1...) custom-call(f32[1024,2048]{1,0:T(8,128)} %slice.166.x_ref, ...), custom_call_target="tpu_custom_call" | custom-call | flops 20000000000 | bytes 40000000 | tf_op jit(solution)/shard_map/pallas_call | solution.py:183
  296.5 5.0 %bitcast_add_fusion.1 = f32[2,2,2,2,32,2048]{5,4,0,1,2,3:T(8,128)} fusion(bf16[2,2,2,2,32,2048]{5,4,0,1,2,3:T(8,128)(2,1)S(1)} %collective-permute-done.1, f32[2,2,2,2,2,32,2048]{6,5,4,3,2,1,0:T(8,128)} %bitcast.172, s32[]{:T(128)S(6)} %select_n.107), kind=kLoop, calls=%fused_computation.58 | loop fusion | flops 2097152 | bytes 10485764 | tf_op jit(solution)/shard_map/add | solution.py:323
  310.1 11.8 %add.297 = f32[1024,2048]{1,0:T(8,128)} add(f32[1024,2048]{1,0:T(8,128)} %get-tuple-element.91, f32[1024,2048]{1,0:T(8,128)} %broadcast_multiply_fusion) | non-fusion elementwise | flops 2097152 | bytes 25165824 | tf_op jit(solution)/shard_map/add | solution.py:282
  321.9 23.0 %multiply_reduce_fusion.3 = (f32[2304]{0:T(1024)S(1)}, f32[2304]{0:T(1024)S(1)}, f32[2304]{0:T(1024)S(1)}, f32[2304]{0:T(1024)S(1)}, f32[2304]{0:T(1024)S(1)}, /*index=5*/f32[1024,2304]{1,0:T(8,128)S(1)}) fusion(f32[1024,2304]{1,0:T(8,128)} %slice.162, f32[1024]{0:T(1024)S(1)} %copy-done.47, f32[1024]{0:T(1024)S(1)} %copy-done.49, f32[1024]{0:T(1024)S(1)} %copy-done.45, ...), kind=kLoop, calls=%fused_computation.15 | loop fusion | flops 54252288 | bytes 47244288 | tf_op jit(solution)/shard_map/transpose(jvp())/reduce_sum | solution.py:230
  345.0 7.5 %multiply_multiply_fusion.2 = (f32[1024,2304]{1,0:T(8,128)S(1)}, f32[1024,2304]{1,0:T(8,128)}, f32[1024,2304]{1,0:T(8,128)}) fusion(f32[1024,2304]{1,0:T(8,128)S(1)} %get-tuple-element.134, f32[1024]{0:T(1024)S(1)} %copy-done.47, f32[2304]{0:T(1024)S(1)} %copy-done.35, f32[1024]{0:T(1024)S(1)} %copy-done.45, f32[2304]{0:T(1024)S(1)} %copy-done.39, ...), kind=kLoop, calls=%fused_computation.21 | loop fusion | flops 14155776 | bytes 37788672 | tf_op jit(solution)/shard_map/transpose(jvp())/mul | solution.py:230
  354.5 10.4 %fusion.5 = bf16[1024,2304]{1,0:T(8,128)(2,1)} fusion(f32[1024,2304]{1,0:T(8,128)} %get-tuple-element.143, f32[1024,2304]{1,0:T(8,128)} %get-tuple-element.144, f32[1024,2304]{1,0:T(8,128)S(1)} %get-tuple-element.142, f32[1024,2304]{1,0:T(8,128)S(1)} %get-tuple-element.134, f32[2304]{0:T(1024)S(1)} %mul.387), kind=kLoop, calls=%fused_computation.10 | loop fusion | flops 11796480 | bytes 42476544 | tf_op jit(solution)/shard_map/convert.2
  365.0 5.1 %fusion.13 = bf16[1024,2432]{1,0:T(8,128)(2,1)} fusion(bf16[1024,32]{1,0:T(8,128)(2,1)S(1)} %get-tuple-element.133, bf16[1024,2304]{1,0:T(8,128)(2,1)} %fusion.5), kind=kLoop, calls=%fused_computation.43 | loop fusion | flops 17432576 | bytes 9764864 | tf_op jit(solution)/shard_map/concatenate | solution.py:392
  373.9 5.0 %fusion.33 = f32[1024,1152]{1,0:T(8,128)S(1)} fusion(bf16[1024,2432]{1,0:T(8,128)(2,1)} %fusion.13, bf16[1024,1024]{1,0:T(8,128)(2,1)S(1)} %copy-done.20, f32[1024]{0:T(1024)S(1)} %copy-done.51, f32[1024]{0:T(1024)S(1)} %copy-done.53), kind=kOutput, calls=%fused_computation.72 | convolution fusion | flops 2420113408 | bytes 9183232 | tf_op jit(solution)/shard_map/dot_general | solution.py:397
  386.5 9.0 %fusion.14 = f32[1024,1024]{1,0:T(8,128)} fusion(bf16[1024,2432]{1,0:T(8,128)(2,1)S(1)} %bitcast.170, bf16[1024,4480]{1,0:T(8,128)(2,1)} %all-gather.3.cloned.1.call-done), kind=kOutput, calls=%fused_computation.44 | convolution fusion | flops 5100273664 | bytes 14155776 | tf_op jit(solution)/shard_map/dot_general | solution.py:403
  395.5 8.1 %fusion.37 = f32[1024,1024]{1,0:T(8,128)S(1)} fusion(f32[1024,1024]{1,0:T(8,128)} %fusion.14, bf16[1024,2048]{1,0:T(8,128)(2,1)S(1)} %copy-done.28, bf16[1024,4480]{1,0:T(8,128)(2,1)} %all-gather.3.cloned.1.call-done), kind=kOutput, calls=%fused_computation.80 | convolution fusion | flops 4296015872 | bytes 16777216 | tf_op jit(solution)/shard_map/dot_general | solution.py:402
  406.1 4.9 collective-permute-done.9
  413.3 5.1 %collective-permute-done.11 = bf16[32,2048]{1,0:T(8,128)(2,1)S(1)} collective-permute-done((bf16[32,2048]{1,0:T(8,128)(2,1)S(1)}, bf16[32,2048]{1,0:T(8,128)(2,1)S(1)}, u32[]{:S(2)}, u32[]{:S(2)}) %collective-permute-start.11) | collective-permute-done | bytes 131104 | tf_op jit(solution)/shard_map/ppermute | solution.py:320
  429.5 13.0 %collective-permute-done.21 = f32[14688]{0:T(1024)S(1)} collective-permute-done((f32[14688]{0:T(1024)S(1)}, f32[14688]{0:T(1024)S(1)}, u32[]{:S(2)}, u32[]{:S(2)}) %collective-permute-start.21) | collective-permute-done | bytes 58784 | tf_op jit(solution)/shard_map/ppermute | solution.py:335
  453.2 3.4 collective-permute-done.24
  462.8 6.5 %collective-permute-done.16 = bf16[2,2,2,32,1280]{4,3,0,1,2:T(8,128)(2,1)S(1)} collective-permute-done((bf16[2,2,2,32,1280]{4,3,0,1,2:T(8,128)(2,1)S(1)}, bf16[2,2,2,32,1280]{4,3,0,1,2:T(8,128)(2,1)S(1)}, u32[]{:S(2)}, u32[]{:S(2)}) %collective-permute-start.16) | collective-permute-done | bytes 655392 | tf_op jit(solution)/shard_map/ppermute | solution.py:320
  483.7 3.9 collective-permute-done.18
  488.4 5.4 %collective-permute-done.19 = bf16[32,1280]{1,0:T(8,128)(2,1)S(1)} collective-permute-done((bf16[32,1280]{1,0:T(8,128)(2,1)S(1)}, bf16[32,1280]{1,0:T(8,128)(2,1)S(1)}, u32[]{:S(2)}, u32[]{:S(2)}) %collective-permute-start.19) | collective-permute-done | bytes 81952 | tf_op jit(solution)/shard_map/ppermute | solution.py:320
  (305 shorter events, 105.1 us)
Async XLA Ops:
  7.2 87.6 %all-gather.3.cloned.1.call-start = ((), (), s32[]{:S(2)}) async-start(), calls=%async_computation | async-start | bytes 9461760 | tf_op jit(solution)/shard_map/all_gather | solution.py:352
  10.8 178.1 %all-gather.5.cloned.1.call-start = ((), (), s32[]{:S(2)}) async-start(), calls=%async_computation.1 | async-start | bytes 4325376 | tf_op jit(solution)/shard_map/all_gather | solution.py:353
  17.0 230.2 %copy-start.52 = (f32[1024]{0:T(1024)}, f32[1024]{0:T(1024)S(1)}, u32[]{:S(2)}) copy-start(f32[1024]{0:T(1024)S(1)} %fusion.102) | copy-start | bytes 12292
  19.2 127.3 %copy-start.4 = (s32[1024,1]{1,0:T(8,128)}, s32[1024,1]{1,0:T(8,128)S(1)}, u32[]{:S(2)}) copy-start(s32[1024,1]{1,0:T(8,128)S(1)} %copy.105.segc_ref) | copy-start | bytes 12292
  20.9 125.1 %copy-start.42 = (f32[8,128]{1,0:T(8,128)}, f32[8,128]{1,0:T(8,128)S(1)}, u32[]{:S(2)}) copy-start(f32[8,128]{1,0:T(8,128)S(1)} %get-tuple-element.157) | copy-start | bytes 12292
  20.9 125.1 %copy-start.54 = (f32[8,128]{1,0:T(8,128)}, f32[8,128]{1,0:T(8,128)S(1)}, u32[]{:S(2)}) copy-start(f32[8,128]{1,0:T(8,128)S(1)} %get-tuple-element.158) | copy-start | bytes 12292
  100.3 146.9 %copy-start.50 = (f32[1024]{0:T(1024)}, f32[1024]{0:T(1024)S(1)}, u32[]{:S(2)}) copy-start(f32[1024]{0:T(1024)S(1)} %mul.392) | copy-start | bytes 12292
  222.9 18.7 %collective-permute-start = (bf16[2,2,2,2,32,2048]{5,4,0,1,3,2:T(8,128)(2,1)}, bf16[2,2,2,2,32,2048]{5,4,0,1,3,2:T(8,128)(2,1)}, u32[]{:S(2)}, u32[]{:S(2)}) collective-permute-start(bf16[2,2,2,2,32,2048]{5,4,0,1,3,2:T(8,128)(2,1)} %fusion.35), channel_id=1, source_target_pairs={{0,2},{2,0},{4,6},{6,4},{8,10},{10,8},{12,14},{14,12},{16,18},{18,... | collective-permute-start | bytes 6291464 | tf_op jit(solution)/shard_map/ppermute | solution.py:320
  245.6 46.6 %collective-permute-start.2 = (bf16[2,2,2,32,2048]{4,3,0,1,2:T(8,128)(2,1)S(1)}, bf16[2,2,2,32,2048]{4,3,0,1,2:T(8,128)(2,1)S(1)}, u32[]{:S(2)}, u32[]{:S(2)}) collective-permute-start(bf16[2,2,2,32,2048]{4,3,0,1,2:T(8,128)(2,1)S(1)} %fusion.42), channel_id=1, source_target_pairs={{0,4},{2,6},{4,0},{6,2},{8,12},{10,14},{12,8},{14,10},{16,20},{18,... | collective-permute-start | bytes 3145736 | tf_op jit(solution)/shard_map/ppermute | solution.py:320
  252.3 44.2 %collective-permute-start.1 = (bf16[2,2,2,2,32,2048]{5,4,0,1,2,3:T(8,128)(2,1)S(1)}, bf16[2,2,2,2,32,2048]{5,4,0,1,2,3:T(8,128)(2,1)S(1)}, u32[]{:S(2)}, u32[]{:S(2)}) collective-permute-start(bf16[2,2,2,2,32,2048]{5,4,0,1,2,3:T(8,128)(2,1)S(1)} %fusion.36), channel_id=1, source_target_pairs={{0,2},{2,0},{4,6},{6,4},{8,10},{10,8},{12,14},{14,12},{16,18},{18,... | collective-permute-start | bytes 6291464 | tf_op jit(solution)/shard_map/ppermute | solution.py:320
  295.8 74.4 %collective-permute-start.4 = (bf16[2,2,32,2048]{3,2,0,1:T(8,128)(2,1)}, bf16[2,2,32,2048]{3,2,0,1:T(8,128)(2,1)}, u32[]{:S(2)}, u32[]{:S(2)}) collective-permute-start(bf16[2,2,32,2048]{3,2,0,1:T(8,128)(2,1)} %fusion.46), channel_id=1, source_target_pairs={{0,1},{1,0},{2,3},{3,2},{4,5},{5,4},{6,7},{7,6},{8,9},{9,8},{10,11... | collective-permute-start | bytes 1572872 | tf_op jit(solution)/shard_map/ppermute | solution.py:320
  308.7 65.2 %collective-permute-start.3 = (bf16[2,2,2,32,2048]{4,3,0,1,2:T(8,128)(2,1)S(1)}, bf16[2,2,2,32,2048]{4,3,0,1,2:T(8,128)(2,1)}, u32[]{:S(2)}, u32[]{:S(2)}) collective-permute-start(bf16[2,2,2,32,2048]{4,3,0,1,2:T(8,128)(2,1)S(1)} %fusion.43), channel_id=1, source_target_pairs={{0,1},{1,0},{2,3},{3,2},{4,5},{5,4},{6,7},{7,6},{8,9},{9,8},{10,11... | collective-permute-start | bytes 3145736 | tf_op jit(solution)/shard_map/ppermute | solution.py:320
  371.8 13.5 %collective-permute-start.6 = (bf16[2,32,2048]{2,1,0:T(8,128)(2,1)S(1)}, bf16[2,32,2048]{2,1,0:T(8,128)(2,1)S(1)}, u32[]{:S(2)}, u32[]{:S(2)}) collective-permute-start(bf16[2,32,2048]{2,1,0:T(8,128)(2,1)S(1)} %fusion.67), channel_id=1, source_target_pairs={{0,8},{2,10},{4,12},{6,14},{8,0},{10,2},{12,4},{14,6},{16,24},{18,... | collective-permute-start | bytes 786440 | tf_op jit(solution)/shard_map/ppermute | solution.py:320
  384.6 18.9 %collective-permute-start.5 = (bf16[2,2,32,2048]{3,2,0,1:T(8,128)(2,1)S(1)}, bf16[2,2,32,2048]{3,2,0,1:T(8,128)(2,1)S(1)}, u32[]{:S(2)}, u32[]{:S(2)}) collective-permute-start(bf16[2,2,32,2048]{3,2,0,1:T(8,128)(2,1)S(1)} %fusion.47), channel_id=1, source_target_pairs={{0,4},{2,6},{4,0},{6,2},{8,12},{10,14},{12,8},{14,10},{16,20},{18,... | collective-permute-start | bytes 1572872 | tf_op jit(solution)/shard_map/ppermute | solution.py:320
  385.3 18.2 %collective-permute-start.10 = (bf16[32,2048]{1,0:T(8,128)(2,1)S(1)}, bf16[32,2048]{1,0:T(8,128)(2,1)S(1)}, u32[]{:S(2)}, u32[]{:S(2)}) collective-permute-start(bf16[32,2048]{1,0:T(8,128)(2,1)S(1)} %fusion.75), channel_id=1, source_target_pairs={{0,16},{2,18},{4,20},{6,22},{8,24},{10,26},{12,28},{14,30},{16,0},... | collective-permute-start | bytes 393224 | tf_op jit(solution)/shard_map/ppermute | solution.py:320
  403.7 7.2 %collective-permute-start.9 = (bf16[2,32,2048]{2,1,0:T(8,128)(2,1)S(1)}, bf16[2,32,2048]{2,1,0:T(8,128)(2,1)S(1)}, u32[]{:S(2)}, u32[]{:S(2)}) collective-permute-start(bf16[2,32,2048]{2,1,0:T(8,128)(2,1)S(1)} %fusion.68), channel_id=1, source_target_pairs={{0,8},{2,10},{4,12},{6,14},{8,0},{10,2},{12,4},{14,6},{16,24},{18,... | collective-permute-start | bytes 786440 | tf_op jit(solution)/shard_map/ppermute | solution.py:320
  405.3 13.8 %collective-permute-start.8 = (bf16[2,2,2,2,32,1152]{5,4,0,1,2,3:T(8,128)(2,1)S(1)}, bf16[2,2,2,2,32,1152]{5,4,0,1,2,3:T(8,128)(2,1)S(1)}, u32[]{:S(2)}, u32[]{:S(2)}) collective-permute-start(bf16[2,2,2,2,32,1152]{5,4,0,1,2,3:T(8,128)(2,1)S(1)} %fusion.41), channel_id=1, source_target_pairs={{0,2},{2,0},{4,6},{6,4},{8,10},{10,8},{12,14},{14,12},{16,18},{18,... | collective-permute-start | bytes 3538952 | tf_op jit(solution)/shard_map/ppermute | solution.py:320
  405.5 15.2 %collective-permute-start.7 = (bf16[2,2,2,2,32,1280]{5,4,0,1,3,2:T(8,128)(2,1)S(1)}, bf16[2,2,2,2,32,1280]{5,4,0,1,3,2:T(8,128)(2,1)S(1)}, u32[]{:S(2)}, u32[]{:S(2)}) collective-permute-start(bf16[2,2,2,2,32,1280]{5,4,0,1,3,2:T(8,128)(2,1)S(1)} %fusion.40), channel_id=1, source_target_pairs={{0,2},{2,0},{4,6},{6,4},{8,10},{10,8},{12,14},{14,12},{16,18},{18,... | collective-permute-start | bytes 3932168 | tf_op jit(solution)/shard_map/ppermute | solution.py:320
  411.0 7.3 %collective-permute-start.11 = (bf16[32,2048]{1,0:T(8,128)(2,1)S(1)}, bf16[32,2048]{1,0:T(8,128)(2,1)S(1)}, u32[]{:S(2)}, u32[]{:S(2)}) collective-permute-start(bf16[32,2048]{1,0:T(8,128)(2,1)S(1)} %fusion.76), channel_id=1, source_target_pairs={{0,16},{2,18},{4,20},{6,22},{8,24},{10,26},{12,28},{14,30},{16,0},... | collective-permute-start | bytes 393224 | tf_op jit(solution)/shard_map/ppermute | solution.py:320
  423.0 3.8 collective-permute-start.20
  425.3 34.3 %collective-permute-start.12 = (bf16[2,2,2,32,1152]{4,3,0,1,2:T(8,128)(2,1)}, bf16[2,2,2,32,1152]{4,3,0,1,2:T(8,128)(2,1)}, u32[]{:S(2)}, u32[]{:S(2)}) collective-permute-start(bf16[2,2,2,32,1152]{4,3,0,1,2:T(8,128)(2,1)} %fusion.45), channel_id=1, source_target_pairs={{0,1},{1,0},{2,3},{3,2},{4,5},{5,4},{6,7},{7,6},{8,9},{9,8},{10,11... | collective-permute-start | bytes 1769480 | tf_op jit(solution)/shard_map/ppermute | solution.py:320
  426.8 15.7 %collective-permute-start.21 = (f32[14688]{0:T(1024)S(1)}, f32[14688]{0:T(1024)S(1)}, u32[]{:S(2)}, u32[]{:S(2)}) collective-permute-start(f32[14688]{0:T(1024)S(1)} %add.321), channel_id=1, source_target_pairs={{0,1},{1,0},{2,3},{3,2},{4,5},{5,4},{6,7},{7,6},{8,9},{9,8},{10,11... | collective-permute-start | bytes 176264 | tf_op jit(solution)/shard_map/ppermute | solution.py:335
  442.5 4.3 collective-permute-start.22
  446.8 4.3 collective-permute-start.23
  451.1 5.5 %collective-permute-start.24 = (f32[14688]{0:T(1024)S(1)}, f32[14688]{0:T(1024)S(1)}, u32[]{:S(2)}, u32[]{:S(2)}) collective-permute-start(f32[14688]{0:T(1024)S(1)} %add.324), channel_id=1, source_target_pairs={{0,16},{2,18},{4,20},{6,22},{8,24},{10,26},{12,28},{14,30},{16,0},... | collective-permute-start | bytes 176264 | tf_op jit(solution)/shard_map/ppermute | solution.py:335
  451.6 17.7 %collective-permute-start.16 = (bf16[2,2,2,32,1280]{4,3,0,1,2:T(8,128)(2,1)S(1)}, bf16[2,2,2,32,1280]{4,3,0,1,2:T(8,128)(2,1)S(1)}, u32[]{:S(2)}, u32[]{:S(2)}) collective-permute-start(bf16[2,2,2,32,1280]{4,3,0,1,2:T(8,128)(2,1)S(1)} %fusion.44), channel_id=1, source_target_pairs={{0,4},{2,6},{4,0},{6,2},{8,12},{10,14},{12,8},{14,10},{16,20},{18,... | collective-permute-start | bytes 1966088 | tf_op jit(solution)/shard_map/ppermute | solution.py:320
  461.3 11.2 %collective-permute-start.13 = (bf16[2,2,32,1152]{3,2,0,1:T(8,128)(2,1)S(1)}, bf16[2,2,32,1152]{3,2,0,1:T(8,128)(2,1)S(1)}, u32[]{:S(2)}, u32[]{:S(2)}) collective-permute-start(bf16[2,2,32,1152]{3,2,0,1:T(8,128)(2,1)S(1)} %fusion.66), channel_id=1, source_target_pairs={{0,4},{2,6},{4,0},{6,2},{8,12},{10,14},{12,8},{14,10},{16,20},{18,... | collective-permute-start | bytes 884744 | tf_op jit(solution)/shard_map/ppermute | solution.py:320
  472.6 5.2 %collective-permute-start.14 = (bf16[2,32,1152]{2,1,0:T(8,128)(2,1)S(1)}, bf16[2,32,1152]{2,1,0:T(8,128)(2,1)S(1)}, u32[]{:S(2)}, u32[]{:S(2)}) collective-permute-start(bf16[2,32,1152]{2,1,0:T(8,128)(2,1)S(1)} %fusion.74), channel_id=1, source_target_pairs={{0,8},{2,10},{4,12},{6,14},{8,0},{10,2},{12,4},{14,6},{16,24},{18,... | collective-permute-start | bytes 442376 | tf_op jit(solution)/shard_map/ppermute | solution.py:320
  473.6 7.1 %collective-permute-start.17 = (bf16[2,2,32,1280]{3,2,0,1:T(8,128)(2,1)S(1)}, bf16[2,2,32,1280]{3,2,0,1:T(8,128)(2,1)S(1)}, u32[]{:S(2)}, u32[]{:S(2)}) collective-permute-start(bf16[2,2,32,1280]{3,2,0,1:T(8,128)(2,1)S(1)} %fusion.65), channel_id=1, source_target_pairs={{0,1},{1,0},{2,3},{3,2},{4,5},{5,4},{6,7},{7,6},{8,9},{9,8},{10,11... | collective-permute-start | bytes 983048 | tf_op jit(solution)/shard_map/ppermute | solution.py:320
  480.9 6.7 %collective-permute-start.18 = (bf16[2,32,1280]{2,1,0:T(8,128)(2,1)S(1)}, bf16[2,32,1280]{2,1,0:T(8,128)(2,1)S(1)}, u32[]{:S(2)}, u32[]{:S(2)}) collective-permute-start(bf16[2,32,1280]{2,1,0:T(8,128)(2,1)S(1)} %fusion.73), channel_id=1, source_target_pairs={{0,8},{2,10},{4,12},{6,14},{8,0},{10,2},{12,4},{14,6},{16,24},{18,... | collective-permute-start | bytes 491528 | tf_op jit(solution)/shard_map/ppermute | solution.py:320
  482.0 6.3 %collective-permute-start.15 = (bf16[32,1152]{1,0:T(8,128)(2,1)S(1)}, bf16[32,1152]{1,0:T(8,128)(2,1)S(1)}, u32[]{:S(2)}, u32[]{:S(2)}) collective-permute-start(bf16[32,1152]{1,0:T(8,128)(2,1)S(1)} %fusion.78), channel_id=1, source_target_pairs={{0,16},{2,18},{4,20},{6,22},{8,24},{10,26},{12,28},{14,30},{16,0},... | collective-permute-start | bytes 221192 | tf_op jit(solution)/shard_map/ppermute | solution.py:320
  487.6 6.2 %collective-permute-start.19 = (bf16[32,1280]{1,0:T(8,128)(2,1)S(1)}, bf16[32,1280]{1,0:T(8,128)(2,1)S(1)}, u32[]{:S(2)}, u32[]{:S(2)}) collective-permute-start(bf16[32,1280]{1,0:T(8,128)(2,1)S(1)} %fusion.77), channel_id=1, source_target_pairs={{0,16},{2,18},{4,20},{6,22},{8,24},{10,26},{12,28},{14,30},{16,0},... | collective-permute-start | bytes 245768 | tf_op jit(solution)/shard_map/ppermute | solution.py:320
  (64 other events, 1348.1 us)
Sparse Core Ops, SparseCore 0:
  11.4 83.3 all-gather.2
  97.8 60.7 all-gather.4
